TPU v7x, 32 devices: a whole 2x2x4 slice. The times are simulated.
32 devices in a mesh: dp: 8 (over z, y), head: 4 (over x, core).
Axes of the slice: x: 2, y: 2, z: 4, core: 2. Of those that a mesh axis runs over, the one named last changes fastest.
Arguments:
- inputs: bfloat16 [32768, 768], P(('dp', 'head')), may hold values from -6 to 6
- segment_ids: int32 [32768], P('dp'), may hold values from 0 to 3, as said below
- norm_gain: float32 [768], replicated, may hold values from 0.5 to 1.5
- up_weight: bfloat16 [768, 2, 1536], P('dp', None, 'head'), may hold values from -0.21875 to 0.21875
- conv_weight: float32 [4, 1536], P(None, 'head'), may hold values from -3 to 3
- conv_bias: float32 [1536], P('head'), may hold values from -3 to 3
- qkv_weight: float32 [3, 384, 4, 4], P(None, 'head'), may hold values from -3 to 3
- gate_weight: bfloat16 [3, 1536, 8], P(None, 'head'), may hold values from -0.078125 to 0.078125
- gate_bias: float32 [2, 4], P(None, 'head'), may hold values from -3 to 8, as said below
- group_gain: float32 [1536], P('head'), may hold values from 0.5 to 1.5
- skip_gain: float32 [1536], P('head'), may hold values from 0.5 to 1.5
- down_weight: bfloat16 [1536, 768], P('head', 'dp'), may hold values from -0.15625 to 0.15625
- out_grad: bfloat16 [32768, 768], P(('dp', 'head')), may hold values from -6 to 6
Outputs:
- output: bfloat16 [32768, 768], P(('dp', 'head'))
- input_grad: float32 [32768, 768], P(('dp', 'head'))
- norm_gain_grad: float32 [768], replicated
- up_weight_grad: float32 [768, 2, 1536], P('dp', None, 'head')
- conv_weight_grad: float32 [4, 1536], P(None, 'head')
- conv_bias_grad: float32 [1536], P('head')
- qkv_weight_grad: float32 [3, 384, 4, 4], P(None, 'head')
- gate_weight_grad: float32 [3, 1536, 8], P(None, 'head')
- gate_bias_grad: float32 [2, 4], P(None, 'head')
- group_gain_grad: float32 [1536], P('head')
- skip_gain_grad: float32 [1536], P('head')
- down_weight_grad: float32 [1536, 768], P('head', 'dp')
Inputs may be any that keep to these rules, and one draw needn't show every extreme that they name: `segment_ids`: within each group of 4096 consecutive tokens the number is constant over each aligned block of 1024 tokens, starts at 0 and rises by 0 or 1 from one block to the next, so that each segment holds 1, 2 or 4 such blocks; some group holds four segments. `gate_bias`: the first row (input gates) lies in -3 to -1, the second (forget gates) in 3 to 8.
All inputs are finite; a program needn't handle non-finite values.
Results may differ from a plain program's by a relative error of at most 0.012.
Values may be sent and summed in bfloat16 or wider, within the bound.
A program may use at most 320 MiB of HBM per device.

v0:
```python
import math
from functools import partial

import jax
import jax.numpy as jnp
from jax import lax
from jax.experimental import pallas as pl
from jax.experimental.pallas import tpu as pltpu
from jax.sharding import PartitionSpec as P

EPS = 1e-05
NEG = -10000.0
CH = 256
HALO = 16
TAPS = 4
F32, BF16 = jnp.float32, jnp.bfloat16
HIGHEST = lax.Precision.HIGHEST


def nn(a, b, **kw):
    return lax.dot_general(a, b, (((1,), (0,)), ((), ())), preferred_element_type=F32, **kw)


def nt(a, b, **kw):
    return lax.dot_general(a, b, (((1,), (1,)), ((), ())), preferred_element_type=F32, **kw)


def tn(a, b, **kw):
    return lax.dot_general(a, b, (((0,), (0,)), ((), ())), preferred_element_type=F32, **kw)


def sigmoid(u):
    return 0.5 * jnp.tanh(0.5 * u) + 0.5


def log_sigmoid(u):
    return jnp.minimum(u, 0.0) - jnp.log(1.0 + jnp.exp(-jnp.abs(u)))


def iota(shape, dim):
    return lax.broadcasted_iota(jnp.int32, shape, dim)


def pick(block, lane):
    return jnp.sum(jnp.where(iota(block.shape, 1) == lane, block, 0.0), axis=1, keepdims=True)


def normalised(rows):
    centred = rows - jnp.mean(rows, axis=1, keepdims=True)
    inv_std = lax.rsqrt(jnp.mean(centred * centred, axis=1, keepdims=True) + EPS)
    return centred * inv_std, inv_std


def row_chunks(total, size):
    return [(r, min(size, total - r)) for r in range(0, total, size)]


def maps_of(pack_ref, cols, rest):
    rows = pack_ref[0, 8:24, cols]
    high = rows.astype(BF16)
    parts = [high]
    if rest:
        parts.append((rows - high.astype(F32)).astype(BF16))
    diagonal = iota((128, 128), 0) // 4 == iota((128, 128), 1) // 4
    made = []
    for part in parts:
        made.append([])
        for m in range(3):
            chosen = jnp.where(iota((16, 128), 0) == 4 * m + iota((16, 128), 1) % 4, 1.0, 0.0).astype(BF16)
            made[-1].append(jnp.where(diagonal, tn(part, chosen), 0.0).astype(BF16))
    return made


def gate_maps(pack_ref, into):
    for m in range(3):
        rows = pack_ref[0, 24 + 8 * m : 32 + 8 * m]
        into[m, 0:16] = jnp.concatenate([rows, jnp.zeros_like(rows)], axis=0).astype(BF16)


def lift_kernel(n_heads, x_ref, halo_ref, gain_ref, seg_ref, pack_ref, w_ref,
                q_ref, k_ref, va_ref, pre_ref, br_ref, og_ref, gates_ref, normt_ref, flags_ref,
                normed, ext, wqk, wv, gw):
    h = pl.program_id(0)
    n, dh = q_ref.shape
    me = lax.axis_index("head")

    @pl.when(h == 0)
    def _():
        gain = jnp.concatenate([gain_ref[j : j + 1] for j in range(gain_ref.shape[0])], axis=1)
        unit, _ = normalised(halo_ref[...].astype(F32))
        normed[0:HALO] = (unit * gain).astype(BF16)
        for r, rows in row_chunks(n, CH):
            unit, _ = normalised(x_ref[r : r + rows].astype(F32))
            scaled = unit * gain
            normed[HALO + r : HALO + r + rows] = scaled.astype(BF16)
            normt_ref[:, r : r + rows] = scaled.T.astype(BF16)
        gates_ref[...] = jnp.zeros_like(gates_ref)
        gw[...] = jnp.zeros_like(gw)
        token = iota(seg_ref.shape, 0) * 128 + iota(seg_ref.shape, 1)

        def segment(at):
            found = jnp.where(token == at, seg_ref[...], 0).astype(F32)
            return jnp.sum(jnp.sum(found, axis=1, keepdims=True), axis=0, keepdims=True)

        own = segment(me * n)
        before = jnp.where((segment(me * n - 1) == own) & (me > 0), 1.0, 0.0)
        after = jnp.where((segment(me * n + n) == own) & (me < n_heads - 1), 1.0, 0.0)
        flags_ref[0:8] = jnp.broadcast_to(before, (8, 128))
        flags_ref[8:16] = jnp.broadcast_to(after, (8, 128))

    gate_maps(pack_ref, gw)
    for b in range(dh // 128):
        (q_high, k_high, v_high), (q_rest, k_rest, v_rest) = maps_of(pack_ref, slice(128 * b, 128 * b + 128), True)
        for at, high, rest in ((0, q_high, q_rest), (128, k_high, k_rest)):
            wqk[b, 0:128, at : at + 128] = high
            wqk[b, 128:256, at : at + 128] = high
            wqk[b, 256:384, at : at + 128] = rest
        wv[b, 0:128] = v_high
        wv[b, 128:256] = v_high
        wv[b, 256:384] = v_rest
    lane = iota((1, 128), 1)
    bias = jnp.where(lane == h, pack_ref[0, 7:8, 0:1], 0.0) + jnp.where(lane == n_heads + h, pack_ref[0, 7:8, 1:2], 0.0)

    w = w_ref.at[0]
    halo = nn(normed[0:HALO], w[:, 0:dh]) * flags_ref[0:1, 0:1]
    ext[0:HALO] = halo
    br_ref[0:HALO] = halo.astype(BF16)
    for r, rows in row_chunks(n, 512):
        lifted = nn(normed[HALO + r : HALO + r + rows], w[...])
        branch = lifted[:, 0:dh]
        ext[HALO + r : HALO + r + rows] = branch
        og_ref[r : r + rows] = lifted[:, dh:].astype(BF16)
        branch_b = branch.astype(BF16)
        br_ref[HALO + r : HALO + r + rows] = branch_b
        pre = pack_ref[0, TAPS : TAPS + 1] + pack_ref[0, 0:1] * branch
        for j in range(1, TAPS):
            pre = pre + pack_ref[0, j : j + 1] * ext[HALO + r - j : HALO + r - j + rows]
        pre_ref[r : r + rows] = pre.astype(BF16)
        conv = pre * sigmoid(pre)
        conv_b = conv.astype(BF16)
        conv_rest = (conv - conv_b.astype(F32)).astype(BF16)
        branch_rest = (branch - branch_b.astype(F32)).astype(BF16)
        for b in range(dh // 128):
            cols = slice(128 * b, 128 * b + 128)
            parts = [conv_b[:, cols], conv_rest[:, cols], conv_b[:, cols]]
            qk = nn(jnp.concatenate(parts, axis=1), wqk[b]).astype(BF16)
            q_ref[r : r + rows, cols] = qk[:, 0:128]
            k_ref[r : r + rows, cols] = qk[:, 128:256]
            parts = [branch_b[:, cols], branch_rest[:, cols], branch_b[:, cols]]
            va_ref[0, r : r + rows, cols] = nn(jnp.concatenate(parts, axis=1), wv[b]).astype(BF16)
        va_ref[0, r : r + rows, dh : dh + 128] = jnp.where(
            iota((rows, 128), 1) == 0, 1.0, 0.0
        ).astype(BF16)
        gates_ref[r : r + rows] += (
            nt(q_ref[r : r + rows], gw[0])
            + nt(k_ref[r : r + rows], gw[1])
            + nt(va_ref[0, r : r + rows, 0:dh], gw[2])
            + bias
        )


def states(h, n_heads, gates_ref, k_ref, va_ref, gcol_ref, grow_ref, sloc, leaving, retain, st, ns):
    n, dh = k_ref.shape

    @pl.when(h == 0)
    def _():
        lower = jnp.where(iota((CH, CH), 0) >= iota((CH, CH), 1), 1.0, 0.0)
        for r, rows in row_chunks(n, CH):
            pre = gates_ref[r : r + rows]
            cum = nn(lower, log_sigmoid(pre), precision=HIGHEST)
            cum = pltpu.roll(cum, 128 - n_heads, 1)
            after = pltpu.roll(pre - cum, n_heads, 1)
            lane = iota((rows, 128), 1)
            both = jnp.where(lane < n_heads, cum, jnp.where(lane < 2 * n_heads, after, 0.0))
            gcol_ref[r : r + rows] = both
            grow_ref[:, r : r + rows] = both.T[0 : grow_ref.shape[0]]

    st[...] = jnp.zeros_like(st)
    ns[...] = jnp.zeros_like(ns)
    chunks = row_chunks(n, CH)
    whole_total = jnp.zeros((1, 1), F32)
    for c, (r, rows) in enumerate(chunks):
        block = gcol_ref[r : r + rows]
        total = pick(block[rows - 8 : rows], h)[7:8]
        whole_total = whole_total + total
        ending = jnp.exp(total + pick(block, n_heads + h))
        weighted = k_ref[r : r + rows].astype(F32) * ending
        st[...] = jnp.exp(total) * st[...] + tn(va_ref[0, r : r + rows, 0:dh], weighted.astype(BF16))
        ns[...] = jnp.exp(total) * ns[...] + jnp.sum(weighted, axis=0, keepdims=True)
        last = c == len(chunks) - 1
        to = leaving.at[h] if last else sloc.at[h, c]
        to[0:dh] = st[...].astype(BF16)
        to[dh : dh + 16] = jnp.where(iota((16, dh), 0) == 0, ns[0:1], 0.0).astype(BF16)
    retain[h] = jnp.broadcast_to(jnp.exp(whole_total), retain.shape[1:])


def decay_of(block, grow_ref, h, n_heads, r, rows, log_scale):
    cum = pick(block, h)
    after = grow_ref[pl.ds(n_heads + h, 1), r : r + rows]
    exponent = jnp.where(
        iota((rows, rows), 0) >= iota((rows, rows), 1), (cum + log_scale) + after, NEG
    )
    return jnp.exp(exponent), cum


def forward_kernel(n_heads, log_scale,
                   x_ref, og_all_ref, gates_ref, flags_ref, q_ref, k_ref, va_ref, gate_ref, pre_ref, pack_ref, w_ref,
                   out_ref, gcol_ref, grow_ref, retain_ref, dng_ref, sttot_ref, gloc_ref, gend_ref, gaug_ref, ogg_ref,
                   dskip_ref, sums_ref,
                   acc, ogt, numer, mixed_s, stb, gt, gn, sloc, leaving, landed, retain, ss, rs):
    step = pl.program_id(0)
    chain = Chain(1, retain, flags_ref[0:1, 0:1], leaving, landed, (ss, rs))
    place = chain.place

    @pl.when(step == 0)
    def _():
        chain.greet()

    @pl.when(step < n_heads)
    def _():
        states(step, n_heads, gates_ref, k_ref, va_ref, gcol_ref, grow_ref, sloc, leaving, retain, gt, gn)

        @pl.when(place == 0)
        def _():
            chain.pump(step)

        @pl.when((place == 1) & (step > 0))
        def _():
            chain.pump(step - 1)

    @pl.when(step >= n_heads)
    def _():
        h = step - n_heads

        @pl.when((place == 1) & (h == 0))
        def _():
            chain.pump(n_heads - 1)

        @pl.when((place > 1) & (h > 0) & (2 * h - 1 < n_heads))
        def _():
            chain.pump(2 * h - 1)

        for c, (r, rows) in enumerate(row_chunks(q_ref.shape[0], CH)):
            span = slice(r, r + rows)
            decay, _ = decay_of(gcol_ref[span], grow_ref, h, n_heads, r, rows, log_scale)
            weights = (nt(q_ref[span], k_ref[span]) * decay).astype(BF16)
            numer[span] = nn(weights, va_ref[0, span])

        @pl.when((place > 1) & (2 * h < n_heads))
        def _():
            chain.pump(2 * h)

        mix(h, n_heads, log_scale, x_ref, og_all_ref, gcol_ref, q_ref, sloc, landed, gate_ref, pre_ref, pack_ref, w_ref,
            out_ref, dng_ref, sttot_ref, gloc_ref, gend_ref, gaug_ref, ogg_ref, dskip_ref, sums_ref,
            acc, ogt, numer, mixed_s, stb, gt, gn)

    @pl.when(step == 2 * n_heads - 1)
    def _():
        retain_ref[...] = retain[...]
        chain.finish()


def mix(h, n_heads, log_scale,
        x_ref, og_all_ref, gcol_ref, q_ref, sloc, landed, gate_ref, pre_ref, pack_ref, w_ref,
        out_ref, dng_ref, sttot_ref, gloc_ref, gend_ref, gaug_ref, ogg_ref, dskip_ref, sums_ref,
        acc, ogt, numer, mixed_s, stb, gt, gn):
    n, dh = q_ref.shape
    gain = pack_ref[0, TAPS + 1 : TAPS + 2]
    skip = pack_ref[0, TAPS + 2 : TAPS + 3]
    down_t = w_ref.at[0]

    @pl.when(h == 0)
    def _():
        acc[...] = jnp.zeros_like(acc)
        for r, rows in row_chunks(n, CH):
            ogt[:, r : r + rows] = og_all_ref[r : r + rows].astype(F32).T.astype(BF16)
        stb[dh + 16 :] = jnp.zeros((stb.shape[0] - dh - 16, dh), BF16)

    prefix = jnp.zeros((1, 1), F32)
    gain_sum = jnp.zeros((1, dh), F32)
    skip_sum = jnp.zeros((1, dh), F32)
    pair_sum = jnp.zeros((1, 1), F32)
    for c, (r, rows) in enumerate(row_chunks(n, CH)):
        span = slice(r, r + rows)
        block = gcol_ref[span]
        total = pick(block[rows - 8 : rows], h)[7:8]
        state = landed[h].astype(F32) * jnp.exp(prefix)
        if c > 0:
            state = state + sloc[h, c - 1].astype(F32)
        prefix = prefix + total
        state_b = state.astype(BF16)
        sttot_ref[0, c] = state_b
        stb[0 : dh + 16] = state_b
        factor = jnp.exp(pick(block, h) + log_scale)
        both = numer[span] + factor * nt(q_ref[span], stb[...])
        denom = both[:, dh : dh + 1]
        r_inv = lax.rsqrt(denom * denom + 1.0)
        unit, inv_std = normalised(both[:, 0:dh] * r_inv)
        gate = gate_ref[span].astype(F32)
        sg = sigmoid(gate)
        silu_gate = gate * sg
        pre = pre_ref[span].astype(F32)
        conv = pre * sigmoid(pre)
        inner = unit * gain + skip * conv
        mixed = (inner * silu_gate).astype(BF16)
        mixed_s[span] = mixed
        acc[span] += nt(mixed, down_t[...])
        mixed_grad = nn(og_all_ref[span], down_t[...])
        hskip = mixed_grad * silu_gate
        ogg_ref[span] = (mixed_grad * inner * (sg * (1.0 + gate * (1.0 - sg)))).astype(BF16)
        dskip_ref[span] = (hskip * skip).astype(BF16)
        skip_sum = skip_sum + jnp.sum(hskip * conv, axis=0, keepdims=True)
        gain_sum = gain_sum + jnp.sum(hskip * unit, axis=0, keepdims=True)
        dhh = hskip * gain
        along = jnp.mean(dhh * unit, axis=1, keepdims=True)
        grad = (inv_std * r_inv) * (dhh - jnp.mean(dhh, axis=1, keepdims=True) - unit * along)
        radial = dh * EPS * along * inv_std * inv_std
        gaug_ref[0, span, 0:dh] = grad.astype(BF16)
        gaug_ref[0, span, dh : dh + 128] = jnp.where(
            iota((rows, 128), 1) == 0, -radial * denom * r_inv * r_inv, 0.0
        ).astype(BF16)
        pair_sum = pair_sum + jnp.sum(radial * r_inv * r_inv, axis=0, keepdims=True)
    sums_ref[0, 0:1] = gain_sum
    sums_ref[0, 1:2] = skip_sum
    sums_ref[0, 2:3] = jnp.broadcast_to(pair_sum, (1, dh))
    sums_ref[0, 3:8] = jnp.zeros((5, dh), F32)

    @pl.when(h == n_heads - 1)
    def _():
        for r, rows in row_chunks(n, CH):
            out_ref[r : r + rows] = (x_ref[r : r + rows].astype(F32) + acc[r : r + rows]).astype(BF16)

    dng_ref[0] = nn(ogt[...], mixed_s[...]).astype(BF16)

    gt[...] = jnp.zeros_like(gt)
    gn[...] = jnp.zeros_like(gn)
    for c, (r, rows) in reversed(list(enumerate(row_chunks(n, CH)))):
        span = slice(r, r + rows)
        block = gcol_ref[span]
        cum = pick(block, h)
        keep = jnp.exp(pick(block[rows - 8 : rows], h)[7:8])
        weighted = q_ref[span].astype(F32) * jnp.exp(cum + log_scale)
        side = gaug_ref[0, span, dh : dh + 128].astype(F32)[:, 0:1]
        gt[...] = keep * gt[...] + tn(gaug_ref[0, span, 0:dh], weighted.astype(BF16))
        gn[...] = keep * gn[...] + jnp.sum(weighted * side, axis=0, keepdims=True)
        to = gloc_ref.at[0, c - 1] if c else gend_ref.at[0]
        to[0:dh] = gt[...].astype(BF16)
        to[dh : dh + 16] = jnp.where(iota((16, dh), 0) == 0, gn[0:1], 0.0).astype(BF16)


def memory_back(h, n_heads, log_scale, chain,
                gates_ref, gcol_ref, grow_ref, q_ref, k_ref, va_ref, gaug_ref, sttot_ref, gloc_ref,
                dq_s, dk_s, dv_s, pg_s, bsum, dk_near, dv_near, stb, gtb, cols, rowsb, across):
    n, dh = q_ref.shape
    chunks = row_chunks(n, CH)

    @pl.when(h == 0)
    def _():
        stb[dh + 16 :] = jnp.zeros((stb.shape[0] - dh - 16, dh), BF16)
        gtb[dh + 16 :] = jnp.zeros((gtb.shape[0] - dh - 16, dh), BF16)
        cols[...] = jnp.zeros_like(cols)
        rowsb[...] = jnp.zeros_like(rowsb)
        across[...] = jnp.zeros_like(across)

    for c, (r, rows) in enumerate(chunks):
        span = slice(r, r + rows)
        stb[0 : dh + 16] = sttot_ref[0, c]
        q, k, va, gaug = q_ref[span], k_ref[span], va_ref[0, span], gaug_ref[0, span]
        decay, cum = decay_of(gcol_ref[span], grow_ref, h, n_heads, r, rows, log_scale)
        weights = nt(q, k) * decay
        wg = nt(gaug, va)
        d_scores = (wg * decay).astype(BF16)
        pair = wg * weights
        dq_far = jnp.exp(cum + log_scale) * nn(gaug, stb[...])
        dq_s[h, span] = (nn(d_scores, k) + dq_far).astype(BF16)
        dk_near[span] = tn(d_scores, q)
        dv_near[span] = tn(weights.astype(BF16), gaug[:, 0:dh])
        row_sum = jnp.sum(pair, axis=1, keepdims=True) + jnp.sum(dq_far * q.astype(F32), axis=1, keepdims=True)
        cols[span] = jnp.where(iota((rows, 128), 1) == h, row_sum, cols[span])
        rowsb[pl.ds(h, 1), span] = jnp.sum(pair, axis=0, keepdims=True)

    @pl.when((chain.place == 1) & (h == 0))
    def _():
        for i in range(1, n_heads):
            chain.pump(i)

    @pl.when(chain.place > 1)
    def _():
        chain.pump(h)

    suffix = jnp.zeros((1, 1), F32)
    for c, (r, rows) in reversed(list(enumerate(chunks))):
        span = slice(r, r + rows)
        block = gcol_ref[span]
        total = pick(block[rows - 8 : rows], h)[7:8]
        after_col = pick(block, n_heads + h)
        grad_state = chain.landed[h].astype(F32) * jnp.exp(suffix)
        if c < len(chunks) - 1:
            grad_state = grad_state + gloc_ref[0, c].astype(F32)
        suffix = suffix + total
        gtb[0 : dh + 16] = grad_state.astype(BF16)
        through = jnp.exp(total) * jnp.sum(
            jnp.sum(sttot_ref[0, c].astype(F32) * grad_state, axis=1, keepdims=True), axis=0, keepdims=True
        )
        k = k_ref[span]
        ending = jnp.exp(total + after_col)
        dk_far = ending * nn(va_ref[0, span], gtb[...])
        dk_s[h, span] = (dk_near[span] + dk_far).astype(BF16)
        dv_s[h, span] = (dv_near[span] + ending * nt(k, gtb[...])[:, 0:dh]).astype(BF16)
        col_far = jnp.sum(dk_far * k.astype(F32), axis=1, keepdims=True)
        cols[span] = jnp.where(iota((rows, 128), 1) == n_heads + h, col_far, cols[span])
        across[c : c + 1] = jnp.where(iota((1, 128), 1) == h, through, across[c : c + 1])

    @pl.when(h == n_heads - 1)
    def _():
        upper = jnp.where(iota((CH, CH), 0) <= iota((CH, CH), 1), 1.0, 0.0)
        strict = jnp.where(iota((CH, CH), 0) > iota((CH, CH), 1), 1.0, 0.0)
        lane = iota((CH, 128), 1)
        bias_sum = jnp.zeros((1, 128), F32)
        for c, (r, rows) in enumerate(chunks):
            span = slice(r, r + rows)
            near_col = rowsb[:, span].T
            far = pltpu.roll(cols[span], 128 - n_heads, 1)
            forget = (
                nn(upper, cols[span] - near_col, precision=HIGHEST)
                + nn(strict, far, precision=HIGHEST)
                + across[c : c + 1]
            )
            pre = gates_ref[span]
            forget = pltpu.roll(forget, n_heads, 1) * sigmoid(-pre)
            grads = jnp.where(
                lane < n_heads, near_col + far, jnp.where(lane < 2 * n_heads, forget, 0.0)
            )
            bias_sum = bias_sum + jnp.sum(grads, axis=0, keepdims=True)
            pg_s[span] = grads.astype(BF16)
        bsum[...] = jnp.where(iota((8, 128), 0) == 0, bias_sum, 0.0)


def lower(h, n_heads,
          x_ref, halo_ref, gain_ref, flags_ref, og_all_ref, normt_ref, pg_ref, bsum_ref, q_ref, k_ref, va_ref,
          dq_s, dk_s, dv_s, pre_ref, br_ref, ogg_ref, dskip_ref,
          pack_ref, w_ref, dng_ref, sums_ref,
          upg_ref, ing_ref, corr_ref, minor_ref,
          nacc, pext, brx, lifted, conv_s, wqk, wv, gw):
    n, dh = q_ref.shape
    link = flags_ref[0:1, 0:1]
    w = w_ref.at[0]

    minor_out = minor_ref
    minor_ref = minor_out.at[pl.ds(h, 1)]
    minor_ref[0, 64:] = jnp.zeros((minor_ref.shape[1] - 64, dh), F32)

    @pl.when(h == 0)
    def _():
        nacc[...] = jnp.zeros_like(nacc)
        ing_ref[...] = jnp.zeros_like(ing_ref)
        pext[0:HALO] = jnp.zeros((HALO, dh), F32)
        pext[HALO + n :] = jnp.zeros((HALO, dh), F32)
        gw[...] = jnp.zeros_like(gw)

    gate_maps(pack_ref, gw)
    for b in range(dh // 128):
        [(q_high, k_high, v_high)] = maps_of(pack_ref, slice(128 * b, 128 * b + 128), False)
        wqk[b, :, 0:128] = q_high
        wqk[b, :, 128:256] = k_high
        wv[b] = v_high

    for r, rows in row_chunks(n + HALO, 208):
        brx[r : r + rows] = br_ref[r : r + rows].astype(F32)

    taps = [jnp.zeros((1, dh), F32) for _ in range(TAPS)]
    bias_sum = jnp.zeros((1, dh), F32)
    for r, rows in row_chunks(n, CH):
        span = slice(r, r + rows)
        pg = pg_ref[span]
        dqt = (dq_s[h, span].astype(F32) + nn(pg, gw[0])).astype(BF16)
        dkt = (dk_s[h, span].astype(F32) + nn(pg, gw[1])).astype(BF16)
        dvt = (dv_s[h, span].astype(F32) + nn(pg, gw[2])).astype(BF16)
        pre = pre_ref[span].astype(F32)
        sg = sigmoid(pre)
        conv_s[span] = (pre * sg).astype(BF16)
        slope = sg * (1.0 + pre * (1.0 - sg))
        dq_s[h, span] = dqt
        dk_s[h, span] = dkt
        dv_s[h, span] = dvt
        for b in range(dh // 128):
            at = slice(128 * b, 128 * b + 128)
            both = jnp.concatenate([dqt[:, at], dkt[:, at]], axis=1)
            conv_grad = nt(both, wqk[b]) + dskip_ref[span, at].astype(F32)
            pext[HALO + r : HALO + r + rows, at] = conv_grad * slope[:, at]
        pre_grad = pext[HALO + r : HALO + r + rows]
        bias_sum = bias_sum + jnp.sum(pre_grad, axis=0, keepdims=True)
        for j in range(TAPS):
            taps[j] = taps[j] + jnp.sum(
                pre_grad * brx[HALO + r - j : HALO + r - j + rows], axis=0, keepdims=True
            )
    for j in range(TAPS):
        minor_ref[0, j : j + 1] = taps[j]
    minor_ref[0, TAPS : TAPS + 1] = bias_sum
    minor_ref[0, TAPS + 1 : 8] = jnp.zeros((8 - TAPS - 1, dh), F32)
    minor_ref[0, 8:16] = sums_ref[0]
    upg_ref[0, :, 2 * dh : 3 * dh] = dng_ref[0]

    halo_grad = jnp.zeros((HALO, dh), F32)
    for j in range(1, TAPS):
        halo_grad = halo_grad + pack_ref[0, j : j + 1] * pext[j : HALO + j]
    halo_b = (halo_grad * link).astype(BF16)
    nacc[0:HALO] += nt(halo_b, w[:, 0:dh])
    for r, rows in row_chunks(n, CH):
        span = slice(r, r + rows)
        grad = jnp.zeros((rows, dh), F32)
        for j in range(TAPS):
            grad = grad + pack_ref[0, j : j + 1] * pext[HALO + r + j : HALO + r + j + rows]
        for b in range(dh // 128):
            at = slice(128 * b, 128 * b + 128)
            lifted[span, at] = (grad[:, at] + nt(dv_s[h, span, at], wv[b])).astype(BF16)
        lifted[span, dh : 2 * dh] = ogg_ref[span]
        ing_ref[span] += nt(lifted[span], w[...])

    unit_halo, std_halo = normalised(halo_ref[...].astype(F32))
    gain = jnp.concatenate([gain_ref[j : j + 1] for j in range(gain_ref.shape[0])], axis=1)
    upg = nn(normt_ref[...], lifted[...])
    upg_ref[0, :, dh : 2 * dh] = upg[:, dh:].astype(BF16)
    upg_ref[0, :, 0:dh] = (upg[:, 0:dh] + tn((unit_halo * gain).astype(BF16), halo_b)).astype(BF16)

    fold = jnp.where(iota((8, 128), 1) % 4 == iota((8, 128), 0), 1.0, 0.0)
    diagonal = iota((128, 128), 0) // 4 == iota((128, 128), 1) // 4
    for b in range(dh // 128):
        at = slice(128 * b, 128 * b + 128)
        qk_grad = tn(conv_s[:, at], jnp.concatenate([dq_s[h, :, at], dk_s[h, :, at]], axis=1))
        v_grad = tn(brx[HALO:, at].astype(BF16), dv_s[h, :, at])
        for m, full in enumerate((qk_grad[:, 0:128], qk_grad[:, 128:256], v_grad)):
            minor_ref[0, 16 + 8 * m : 24 + 8 * m, at] = nt(fold, jnp.where(diagonal, full, 0.0), precision=HIGHEST)
    minor_ref[0, 40:48] = tn(pg_ref[...], q_ref[...])[0:8]
    minor_ref[0, 48:56] = tn(pg_ref[...], k_ref[...])[0:8]
    minor_ref[0, 56:64] = tn(pg_ref[...], va_ref[0, :, 0:dh])[0:8]

    @pl.when(h == n_heads - 1)
    def _():
        def back(normed_grad, unit, inv_std):
            scaled = normed_grad * gain
            return inv_std * (
                scaled
                - jnp.mean(scaled, axis=1, keepdims=True)
                - unit * jnp.mean(scaled * unit, axis=1, keepdims=True)
            )

        corr_ref[...] = back(nacc[0:HALO], unit_halo, std_halo)
        total = jnp.sum(nacc[0:HALO] * unit_halo, axis=0, keepdims=True)
        for r, rows in row_chunks(n, CH):
            unit, inv_std = normalised(x_ref[r : r + rows].astype(F32))
            grads = ing_ref[r : r + rows]
            total = total + jnp.sum(grads * unit, axis=0, keepdims=True)
            ing_ref[r : r + rows] = og_all_ref[r : r + rows].astype(F32) + back(grads, unit, inv_std)
        for i in range(n_heads):
            minor_out[i, 66:67] = jnp.broadcast_to(bsum_ref[0:1, n_heads + i : n_heads + i + 1], (1, dh))
            for j in range(total.shape[1] // dh):
                minor_out[i, 64 + j : 65 + j] = total[:, dh * j : dh * j + dh]


def backward_kernel(n_heads, log_scale,
                    x_ref, halo_ref, gain_ref, flags_ref, og_all_ref, normt_ref, gates_ref, gcol_ref, grow_ref, retain_ref,
                    gend_ref, q_ref, k_ref, va_ref, gaug_ref, sttot_ref, gloc_ref, pre_ref, br_ref, ogg_ref, dskip_ref,
                    pack_ref, w_ref, dng_ref, sums_ref,
                    upg_ref, ing_ref, corr_ref, minor_ref,
                    dq_s, dk_s, dv_s, pg_s, bsum, stb, gtb, cols, rowsb, across,
                    nacc, pext, brx, lifted, conv_s, wqk, wv, gw, leaving, landed, ss, rs):
    step = pl.program_id(0)
    chain = Chain(-1, retain_ref, flags_ref[8:9, 0:1], leaving, landed, (ss, rs))

    @pl.when(step == 0)
    def _():
        chain.greet()
        leaving[...] = gend_ref[...]

        @pl.when(chain.place == 0)
        def _():
            for i in range(n_heads):
                chain.pump(i)

        @pl.when(chain.place == 1)
        def _():
            chain.pump(0)

    dh = q_ref.shape[1]
    near_k, near_v = ing_ref.at[:, 0:dh], ing_ref.at[:, dh : 2 * dh]

    @pl.when(step < n_heads)
    def _():
        memory_back(step, n_heads, log_scale, chain, gates_ref, gcol_ref, grow_ref, q_ref, k_ref, va_ref, gaug_ref,
                    sttot_ref, gloc_ref, dq_s, dk_s, dv_s, pg_s, bsum, near_k, near_v, stb, gtb, cols, rowsb, across)

    @pl.when(step >= n_heads)
    def _():
        lower(step - n_heads, n_heads, x_ref, halo_ref, gain_ref, flags_ref, og_all_ref, normt_ref, pg_s, bsum, q_ref,
              k_ref, va_ref, dq_s, dk_s, dv_s, pre_ref, br_ref, ogg_ref, dskip_ref, pack_ref, w_ref, dng_ref, sums_ref,
              upg_ref, ing_ref, corr_ref, minor_ref, nacc, pext, brx, lifted, conv_s, wqk, wv, gw)

    @pl.when(step == 2 * n_heads - 1)
    def _():
        chain.finish()


class Specs:
    def __init__(self, heads, rounds=2):
        self.heads, self.steps = heads, heads * rounds
        self.index = dict(
            both=lambda s: lax.rem(s, heads),
            first=lambda s: jnp.minimum(s, heads - 1),
            second=lambda s: jnp.maximum(s - heads, 0),
        )

    def whole(self, *shape):
        return pl.BlockSpec(shape, lambda s: (0,) * len(shape), pipeline_mode=pl.Buffered(1))

    def cols(self, when, rows, cols):
        index = self.index[when]
        return pl.BlockSpec((None, rows, cols), lambda s: (index(s), 0, 0))

    def lead(self, when, *shape, last=0):
        index = self.index[when]
        return pl.BlockSpec((1, *shape), lambda s: (index(s),) + (0,) * (len(shape) - 1) + (last,))


def params(**kw):
    return pltpu.CompilerParams(dimension_semantics=("arbitrary",), vmem_limit_bytes=62 << 20, **kw)


def sds(shape, dtype):
    return jax.ShapeDtypeStruct(shape, dtype)


def shifted(x, by):
    heads = lax.axis_size("head")
    pairs = [(i, i + by) for i in range(heads) if 0 <= i + by < heads]
    return lax.ppermute(x, "head", pairs)


MESH = pl.DeviceIdType.MESH


class Place:
    def __init__(self):
        dp, head = lax.axis_index("dp"), lax.axis_index("head")
        self.z, self.y = lax.div(dp, 2), lax.rem(dp, 2)
        self.x, self.c = lax.div(head, 2), lax.rem(head, 2)

    def along_z(self, k):
        z = self.z
        return (z, z + 1 - 2 * lax.rem(z, 2), lax.rem(z + 2, 4), 3 - z)[k]

    def device(self, k=0, fy=0, fx=0, fc=0):
        y, x, c = (1 - v if f else v for v, f in ((self.y, fy), (self.x, fx), (self.c, fc)))
        return (self.along_z(k) * 2 + y, x * 2 + c)

    def head(self, fx=0, fc=0):
        return (1 - self.x if fx else self.x) * 2 + (1 - self.c if fc else self.c)

    def rows(self, k, fy, size):
        y = 1 - self.y if fy else self.y
        return pl.multiple_of((self.along_z(k) * 2 + y) * size, 16)


NEIGHBOURS = (dict(fc=1), dict(fx=1), dict(fx=1, fc=1), dict(fy=1), dict(k=1), dict(k=2), dict(k=3))


def greet(devices):
    barrier = pltpu.get_barrier_semaphore()
    for device in devices:
        pl.semaphore_signal(barrier, inc=1, device_id=device, device_id_type=MESH)
    pl.semaphore_wait(barrier, len(devices))


def remote(src, dst, sems, at, device):
    send, recv = sems
    return pltpu.make_async_remote_copy(
        src_ref=src, dst_ref=dst, send_sem=send.at[at], recv_sem=recv.at[at], device_id=device, device_id_type=MESH
    )


class Gather:
    SEMAPHORES = ((2, 3), (2, 3), (2, 4), (2, 4), (2, 4, 2), (2, 4, 2), (2, 4, 4), (2, 4, 4))
    FLIPS = ((dict(fx=1), dict(fy=1)), (dict(fy=1), dict(fx=1)))

    def __init__(self, here, shard, w, sems):
        self.here, self.shard, self.w = here, shard, w
        self.z, self.f, self.s, self.d = (tuple(sems[i : i + 2]) for i in (0, 2, 4, 6))
        self.rows = shard.shape[0]
        self.started = []

    def block(self, p, k=0, fy=0, fx=0, fc=0):
        half = self.rows // 2
        return self.w.at[self.here.head(fx, fc), pl.ds(self.here.rows(k, fy, self.rows) + half * p, half)]

    def send(self, src, dst, sems, at, to):
        copy = remote(src, dst, sems, at, self.here.device(**to))
        copy.start()
        self.started.append(copy)

    def arrived(self, dst, sems, at):
        remote(dst, dst, sems, at, self.here.device(fc=1)).wait_recv()

    def begin(self):
        half = self.rows // 2
        for p in (0, 1):
            mine = self.shard.at[pl.ds(half * p, half)]
            first, second = self.FLIPS[p]
            self.send(mine, self.block(p), self.z, (p, 0), dict(k=1))
            self.send(mine, self.block(p), self.f, (p, 0), first)
        for p in (0, 1):
            mine = self.shard.at[pl.ds(half * p, half)]
            first, second = self.FLIPS[p]
            for k in (2, 3):
                self.send(mine, self.block(p), self.z, (p, k - 1), dict(k=k))
            self.send(mine, self.block(p), self.s, (p, 0, 0), second)
            self.send(mine, self.block(p), self.d, (p, 0, 0), dict(fc=1))

    def from_z(self, k):
        for p in (0, 1):
            first, second = self.FLIPS[p]
            block = self.block(p, k)
            self.arrived(block, self.z, (p, k - 1))
            self.send(block, block, self.f, (p, k), first)
            self.send(block, block, self.s, (p, k, 0), second)
            self.send(block, block, self.d, (p, k, 0), dict(fc=1))

    def from_first(self, k):
        for p in (0, 1):
            first, second = self.FLIPS[p]
            block = self.block(p, k, **first)
            self.arrived(block, self.f, (p, k))
            self.send(block, block, self.s, (p, k, 1), second)
            self.send(block, block, self.d, (p, k, 1), dict(fc=1))

    def from_second(self, k):
        for i in (0, 1):
            for p in (0, 1):
                first, second = self.FLIPS[p]
                block = self.block(p, k, **(dict(**first, **second) if i else second))
                self.arrived(block, self.s, (p, k, i))
                self.send(block, block, self.d, (p, k, 2 + i), dict(fc=1))

    def from_core(self, k):
        for p in (0, 1):
            first, second = self.FLIPS[p]
            for i, over in enumerate((dict(), first, second, dict(**first, **second))):
                self.arrived(self.block(p, k, fc=1, **over), self.d, (p, k, i))

    def run(self):
        self.begin()
        self.from_first(0)
        for k in (1, 2, 3):
            self.from_z(k)
            self.from_second(k - 1)
            self.from_first(k)
        self.from_second(3)
        for k in range(4):
            self.from_core(k)
        for copy in self.started:
            copy.wait_send()


def gather_kernel(up_raw, down, taps, conv_bias, group, skip, gate_bias, maps, gates, x, w, pack_all, halo,
                  shard, pack, rows_s, local_sem, ms, mr, *sems):
    here = Place()
    n = x.shape[0]
    dh = pack.shape[1]
    rows = shard.shape[0]
    shard[:, 0:dh] = up_raw[:, 0]
    shard[:, dh : 2 * dh] = up_raw[:, 1]
    shard[:, 2 * dh :] = down[...]
    fill_pack(taps, conv_bias, group, skip, gate_bias, maps, gates, pack, rows_s)
    copies = [pltpu.make_async_copy(pack, pack_all.at[here.head()], local_sem.at[0]),
              pltpu.make_async_copy(shard, w.at[here.head(), pl.ds(here.rows(0, 0, rows), rows)], local_sem.at[1])]
    for copy in copies:
        copy.start()
    greet([here.device(**to) for to in NEIGHBOURS])
    small = []
    for i, to in enumerate(NEIGHBOURS[:3]):
        small.append(remote(pack, pack_all.at[here.head()], (ms, mr), i, here.device(**to)))
    after = (here.z * 2 + here.y, lax.rem(here.head() + 1, 4))
    small.append(remote(x.at[pl.ds(n - HALO, HALO)], halo, (ms, mr), 3, after))
    for copy in small:
        copy.start()
    Gather(here, shard, w, sems).run()
    for i, to in enumerate(NEIGHBOURS[:3]):
        from_them = pack_all.at[here.head(to.get("fx", 0), to.get("fc", 0))]
        remote(from_them, from_them, (ms, mr), i, here.device(fc=1)).wait_recv()
    remote(halo, halo, (ms, mr), 3, here.device(fc=1)).wait_recv()
    for copy in small:
        copy.wait_send()
    for copy in copies:
        copy.wait()


def fill_pack(taps, conv_bias, group, skip, gate_bias, maps, gates, pack, rows_s):
    dh = pack.shape[1]
    pack[0:TAPS] = taps[...]
    for i, ref in enumerate((conv_bias, group, skip)):
        for j in range(dh // 128):
            pack[TAPS + i : TAPS + i + 1, 128 * j : 128 * j + 128] = ref[j : j + 1]
    lane = iota((1, dh), 1)
    pack[7:8] = jnp.where(lane == 0, gate_bias[0:1, 0:1], jnp.where(lane == 1, gate_bias[0:1, 1:2], 0.0))
    rows_s[...] = jnp.zeros_like(rows_s)
    for m in range(3):
        for i in range(4):
            rows_s[16 * m + 4 * i : 16 * m + 4 * i + 4, 0 : dh // 4] = maps[m, i]
        pack[24 + 8 * m : 32 + 8 * m] = gates[m].astype(F32)
    wide = nn(rows_s[...], jnp.where(iota((128, dh), 1) // 4 == iota((128, dh), 0), 1.0, 0.0), precision=HIGHEST)
    for m in range(3):
        rows = jnp.zeros((4, dh), F32)
        for i in range(4):
            rows = jnp.where(iota((4, dh), 1) % 4 == i, wide[16 * m + 4 * i : 16 * m + 4 * i + 4], rows)
        pack[8 + 4 * m : 12 + 4 * m] = rows
    pack[20:24] = jnp.zeros((4, dh), F32)


def gathered(up_weight, down, small, x, heads):
    dp = lax.axis_size("dp")
    n, d = x.shape
    vmem = pl.BlockSpec(memory_space=pltpu.VMEM)
    rows, _, dh = up_weight.shape
    if not by_hand(rows):
        up = up_weight.reshape(rows, 2 * dh)
        pack = pl.pallas_call(
            fill_pack, out_shape=sds((48, dh), F32), in_specs=[vmem] * 7, out_specs=vmem,
            scratch_shapes=[pltpu.VMEM((48, 128), F32)], name="pack",
        )(*small)

        def all_of(shard):
            w = lax.all_gather(shard, ("dp", "head"), axis=0)
            w = w.reshape(dp, heads, *shard.shape).transpose(1, 0, 2, 3)
            return w.reshape(heads, dp * shard.shape[0], shard.shape[1])

        w = all_of(jnp.concatenate([up, down], axis=1))
        return w, lax.all_gather(pack, "head", axis=0), shifted(x[n - HALO :], 1)
    sem = pltpu.SemaphoreType.DMA
    anywhere = pl.BlockSpec(memory_space=pl.ANY)
    return pl.pallas_call(
        gather_kernel,
        out_shape=[sds((heads, dp * rows, 3 * dh), BF16), sds((heads, 48, dh), F32), sds((HALO, d), BF16)],
        in_specs=[vmem, vmem, *[vmem] * 7, anywhere],
        out_specs=[anywhere] * 3,
        scratch_shapes=[pltpu.VMEM((rows, 3 * dh), BF16), pltpu.VMEM((48, dh), F32), pltpu.VMEM((48, 128), F32),
                        sem((2,)), sem((4,)), sem((4,)), *(sem(shape) for shape in Gather.SEMAPHORES)],
        compiler_params=pltpu.CompilerParams(collective_id=0, has_side_effects=True),
        name="gather",
    )(up_weight, down, *small, x)


def by_hand(rows):
    return lax.axis_size("dp") == 8 and lax.axis_size("head") == 4 and rows % 32 == 0


def scatter_kernel(part, minor, corr, total, minor_total, corr_in,
                   own, r0, r1a, r1b, r2, r3, m0, m1, n0, n1,
                   load, s0, t0, s1, t1, s2, t2, s3, t3, ms, mr):
    here = Place()
    rows = total.shape[0]
    half = rows // 2
    spans = (pl.ds(0, half), pl.ds(half, half))
    order = (1, 2, 3, 0)
    corners = ((1, 1), (1, 0), (0, 1), (0, 0))

    def block(k, fx, fy, fc):
        return part.at[here.head(fx, fc), pl.ds(here.rows(k, fy, rows), rows)]

    loads = {}
    for k in order:
        for fx, fy in corners:
            loads[k, fx, fy] = pltpu.make_async_copy(block(k, fx, fy, 0), own.at[fx, k, fy], load.at[fx, k, fy])
            loads[k, fx, fy].start()
    small = [pltpu.make_async_copy(minor.at[here.head(fx)], m0.at[fx], load.at[fx, 4, 0]) for fx in (0, 1)]
    for copy in small:
        copy.start()
    greet([here.device(**to) for to in NEIGHBOURS])
    started = []

    def send(src, dst, sems, at, to):
        copy = remote(src, dst, sems, at, to if isinstance(to, tuple) else here.device(**to))
        copy.start()
        started.append(copy)

    def arrived(dst, sems, at):
        remote(dst, dst, sems, at, here.device(fc=1)).wait_recv()

    def add(into, other):
        into[...] = (into[...].astype(F32) + other[...].astype(F32)).astype(into.dtype)

    def first(k):
        for fx, fy in corners:
            loads[k, fx, fy].wait()
            arrived(r0.at[fx, k, fy], (s0, t0), (fx, k, fy))
            add(own.at[fx, k, fy], r0.at[fx, k, fy])
            if fy:
                send(own.at[fx, k, 1, spans[0]], r1a.at[fx, k], (s1, t1), (0, fx, k), dict(fy=1))
            if fx:
                send(own.at[1, k, fy, spans[1]], r1b.at[fy, k], (s1, t1), (1, fy, k), dict(fx=1))

    def second(k):
        for f in (1, 0):
            arrived(r1a.at[f, k], (s1, t1), (0, f, k))
            add(own.at[f, k, 0, spans[0]], r1a.at[f, k])
            if f:
                send(own.at[1, k, 0, spans[0]], r2.at[0, k], (s2, t2), (0, k), dict(fx=1))
            arrived(r1b.at[f, k], (s1, t1), (1, f, k))
            add(own.at[0, k, f, spans[1]], r1b.at[f, k])
            if f:
                send(own.at[0, k, 1, spans[1]], r2.at[1, k], (s2, t2), (1, k), dict(fy=1))

    def third(k):
        for p in (0, 1):
            arrived(r2.at[p, k], (s2, t2), (p, k))
            add(own.at[0, k, 0, spans[p]], r2.at[p, k])
            if k:
                send(own.at[0, k, 0, spans[p]], r3.at[p, k - 1], (s3, t3), (p, k - 1), dict(k=k))

    send(corr, corr_in, (ms, mr), 6, (here.z * 2 + here.y, lax.rem(here.head() + 3, 4)))
    for fx in (0, 1):
        send(minor.at[here.head(fx, 1)], n0.at[fx], (ms, mr), fx, dict(fc=1))
    for k in order:
        for fx, fy in corners:
            send(block(k, fx, fy, 1), r0.at[fx, k, fy], (s0, t0), (fx, k, fy), dict(fc=1))
    for fx in (0, 1):
        small[fx].wait()
        arrived(n0.at[fx], (ms, mr), fx)
        add(m0.at[fx], n0.at[fx])
    send(m0.at[1], n1.at[0], (ms, mr), 2, dict(fx=1))
    first(1)
    first(2)
    second(1)
    arrived(n1.at[0], (ms, mr), 2)
    m1[0] = m0[0] + n1[0]
    send(m1.at[0], n1.at[1], (ms, mr), 3, dict(fy=1))
    first(3)
    second(2)
    third(1)
    arrived(n1.at[1], (ms, mr), 3)
    m1[1] = m1[0] + n1[1]
    send(m1.at[1], n1.at[2], (ms, mr), 4, dict(k=1))
    first(0)
    second(3)
    third(2)
    arrived(n1.at[2], (ms, mr), 4)
    m1[2] = m1[1] + n1[2]
    send(m1.at[2], n1.at[3], (ms, mr), 5, dict(k=2))
    second(0)
    third(3)
    third(0)
    for p in (0, 1):
        summed = own[0, 0, 0, spans[p]].astype(F32)
        for k in range(3):
            arrived(r3.at[p, k], (s3, t3), (p, k))
            summed = summed + r3[p, k].astype(F32)
        total[spans[p]] = summed
    arrived(n1.at[3], (ms, mr), 5)
    minor_total[...] = m1[2] + n1[3]
    arrived(corr_in, (ms, mr), 6)
    for copy in started:
        copy.wait_send()


def scattered(part, minor, corr):
    dp = lax.axis_size("dp")
    heads, d, cols = part.shape
    rows = d // dp
    if not by_hand(rows):
        part = lax.psum_scatter(part, "head", scatter_dimension=0, tiled=True)
        part = lax.psum_scatter(part, "dp", scatter_dimension=1, tiled=True)[0].astype(F32)
        minor = lax.psum(lax.psum_scatter(minor, "head", scatter_dimension=0, tiled=True), "dp")[0]
        return part, minor, shifted(corr, -1)
    sem = pltpu.SemaphoreType.DMA
    half = rows // 2
    lines = minor.shape[1:]
    vmem = pl.BlockSpec(memory_space=pltpu.VMEM)
    return pl.pallas_call(
        scatter_kernel,
        out_shape=[sds((rows, cols), F32), sds(lines, F32), sds(corr.shape, F32)],
        in_specs=[pl.BlockSpec(memory_space=pl.ANY)] * 3,
        out_specs=[vmem] * 3,
        scratch_shapes=[
            pltpu.VMEM((2, 4, 2, rows, cols), BF16), pltpu.VMEM((2, 4, 2, rows, cols), BF16),
            pltpu.VMEM((2, 4, half, cols), BF16), pltpu.VMEM((2, 4, half, cols), BF16),
            pltpu.VMEM((2, 4, half, cols), BF16), pltpu.VMEM((2, 3, half, cols), BF16),
            pltpu.VMEM((2, *lines), F32), pltpu.VMEM((3, *lines), F32),
            pltpu.VMEM((2, *lines), F32), pltpu.VMEM((4, *lines), F32),
            sem((2, 5, 2)), sem((2, 4, 2)), sem((2, 4, 2)), sem((2, 2, 4)), sem((2, 2, 4)), sem((2, 4)), sem((2, 4)),
            sem((2, 3)), sem((2, 3)), sem((7,)), sem((7,)),
        ],
        compiler_params=pltpu.CompilerParams(collective_id=1, has_side_effects=True, vmem_limit_bytes=60 << 20),
        name="scatter",
    )(part, minor, corr)


def finish_kernel(n_heads, total, minor, corr, ing, output, up, down, conv_w, conv_b, maps, gate_w, gate_b, group, skip, gain, ing_out, out):
    dh = minor.shape[1]
    up[:, 0] = total[:, 0:dh]
    up[:, 1] = total[:, dh : 2 * dh]
    down[...] = total[:, 2 * dh :]
    conv_w[...] = minor[0:TAPS]
    for j in range(dh // 128):
        at = slice(128 * j, 128 * j + 128)
        for ref, row in ((conv_b, TAPS), (group, 8), (skip, 9)):
            ref[j : j + 1] = minor[row : row + 1, at]
        for i in range(gain.shape[0] * 128 // dh):
            gain[dh // 128 * i + j : dh // 128 * i + j + 1] = minor[64 + i : 65 + i, at]
    for m in range(3):
        gate_w[m] = minor[40 + 8 * m : 48 + 8 * m]
    for i in range(4):
        chosen = jnp.where(iota((dh, 128), 0) == 4 * iota((dh, 128), 1) + i, 1.0, 0.0)
        rows = nn(minor[16:40], chosen, precision=HIGHEST)
        for m in range(3):
            maps[m, i] = rows[8 * m : 8 * m + 4, 0 : dh // 4]
    gate_b[0:1, 0:1] = minor[10:11, 0:1]
    gate_b[0:1, 1:2] = minor[66:67, 0:1]
    last = lax.axis_index("head") == n_heads - 1
    ing_out[...] = ing[...] + jnp.where(last, 0.0, corr[...])


class Chain:
    def __init__(self, by, retain, linked, leaving, landed, sems):
        self.dp, head = lax.axis_index("dp"), lax.axis_index("head")
        self.heads = lax.axis_size("head")
        self.ahead, self.behind = lax.rem(head + 1, self.heads), lax.rem(head + self.heads - 1, self.heads)
        self.place = head if by > 0 else self.heads - 1 - head
        self.to = (self.dp, self.ahead if by > 0 else self.behind)
        self.retain, self.linked, self.leaving, self.landed, self.sems = retain, linked, leaving, landed, sems

    def greet(self):
        greet([(self.dp, self.ahead), (self.dp, self.behind)])

    def copy(self, i):
        return remote(self.leaving.at[i], self.landed.at[i], self.sems, i, self.to)

    def pump(self, i):
        @pl.when(self.place != 0)
        def _():
            self.copy(i).wait_recv()
            entering = self.landed[i].astype(F32) * self.linked
            self.landed[i] = entering.astype(BF16)
            self.leaving[i] = (self.leaving[i].astype(F32) + entering * self.retain[i, 0:1, 0:1]).astype(BF16)

        @pl.when(self.place == 0)
        def _():
            self.landed[i] = jnp.zeros(self.landed.shape[1:], BF16)

        @pl.when(self.place != self.heads - 1)
        def _():
            self.copy(i).start()

    def finish(self):
        @pl.when(self.place != self.heads - 1)
        def _():
            for i in range(self.heads):
                self.copy(i).wait_send()


def local(inputs, segment_ids, norm_gain, up_weight, conv_weight, conv_bias, qkv_weight,
          gate_weight, gate_bias, group_gain, skip_gain, down_weight, out_grad):
    H = lax.axis_size("head")
    n, d = inputs.shape
    dh = up_weight.shape[2]
    srows = dh + 16
    nch = n // CH
    log_scale = -0.5 * math.log(dh)

    small = (conv_weight, conv_bias.reshape(-1, 128), group_gain.reshape(-1, 128), skip_gain.reshape(-1, 128), gate_bias.T,
             qkv_weight.transpose(0, 2, 3, 1), gate_weight.transpose(0, 2, 1))
    w_all, pack, halo = gathered(up_weight, down_weight.T, small, inputs, H)
    gain = norm_gain.reshape(-1, 128)
    seg = segment_ids.reshape(-1, 128)

    def call(kernel, name, rounds, ins, outs, scratch, **kw):
        return pl.pallas_call(
            kernel, grid=(H * rounds,), out_shape=[o[0] for o in outs], in_specs=[i[1] for i in ins],
            out_specs=[o[1] for o in outs], scratch_shapes=scratch, compiler_params=params(**kw), name=name,
        )(*[i[0] for i in ins])

    sp = Specs(H, 1)
    per_head = sp.lead("both", *pack.shape[1:])
    cols_b = (sds((H, n, dh), BF16), sp.cols("both", n, dh))
    whole = lambda a: (a, sp.whole(*a.shape))
    q, k, va, pre, br, og, gates, normt, flags = call(
        partial(lift_kernel, H), "lift", 1,
        [whole(inputs), whole(halo), whole(gain), whole(seg), (pack, per_head), (w_all, sp.lead("both", d, 2 * dh))],
        [cols_b, cols_b, (sds((H, n, dh + 128), BF16), sp.lead("both", n, dh + 128)), cols_b,
         (sds((H, n + HALO, dh), BF16), sp.cols("both", n + HALO, dh)), cols_b,
         whole(sds((n, 128), F32)), whole(sds((d, n), BF16)), whole(sds((16, 128), F32))],
        [pltpu.VMEM((n + HALO, d), BF16), pltpu.VMEM((n + HALO, dh), F32), pltpu.VMEM((dh // 128, 384, 256), BF16),
         pltpu.VMEM((dh // 128, 384, 128), BF16), pltpu.VMEM((3, 128, dh), BF16)],
    )

    sp = Specs(H)
    sem = pltpu.SemaphoreType.DMA((H,))
    state = pltpu.VMEM((H, srows, dh), BF16)
    late = lambda a: (a, sp.cols("second", n, dh))
    output, gcol, grow, retain, dng, sttot, gloc, gend, gaug, ogg, dskip, sums = call(
        partial(forward_kernel, H, log_scale), "forward", 2,
        [whole(inputs), whole(out_grad), whole(gates), whole(flags), late(q), (k, sp.cols("both", n, dh)),
         (va, sp.lead("both", n, dh + 128)), late(og), late(pre), (pack, sp.lead("second", *pack.shape[1:])),
         (w_all, sp.lead("second", d, dh, last=2))],
        [whole(sds((n, d), BF16)), whole(sds((n, 128), F32)), whole(sds((8, n), F32)), whole(sds((H, 8, 128), F32)),
         (sds((H, d, dh), BF16), sp.lead("second", d, dh)),
         (sds((H, nch, srows, dh), BF16), sp.lead("second", nch, srows, dh)),
         (sds((H, nch - 1, srows, dh), BF16), sp.lead("second", nch - 1, srows, dh)),
         (sds((H, srows, dh), BF16), sp.lead("second", srows, dh)),
         (sds((H, n, dh + 128), BF16), sp.lead("second", n, dh + 128)), late(sds((H, n, dh), BF16)),
         late(sds((H, n, dh), BF16)), (sds((H, 8, dh), F32), sp.lead("second", 8, dh))],
        [pltpu.VMEM((n, d), F32), pltpu.VMEM((d, n), BF16), pltpu.VMEM((n, dh + 128), F32), pltpu.VMEM((n, dh), BF16),
         pltpu.VMEM((dh + 128, dh), BF16), pltpu.VMEM((dh, dh), F32), pltpu.VMEM((1, dh), F32),
         pltpu.VMEM((H, nch - 1, srows, dh), BF16), state, state, pltpu.VMEM((H, 8, 128), F32), sem, sem],
        collective_id=2, has_side_effects=True,
    )

    early = lambda a, *shape: (a, sp.lead("first", *shape))
    grads, ing, corr, minor = call(
        partial(backward_kernel, H, log_scale), "backward", 2,
        [whole(inputs), whole(halo), whole(gain), whole(flags), whole(out_grad), whole(normt), whole(gates), whole(gcol),
         whole(grow), whole(retain), whole(gend), (q, sp.cols("both", n, dh)), (k, sp.cols("both", n, dh)),
         (va, sp.lead("both", n, dh + 128)), early(gaug, n, dh + 128), early(sttot, nch, srows, dh),
         early(gloc, nch - 1, srows, dh), late(pre), (br, sp.cols("second", n + HALO, dh)), late(ogg), late(dskip),
         (pack, sp.lead("second", *pack.shape[1:])), (w_all, sp.lead("second", d, 2 * dh)),
         (dng, sp.lead("second", d, dh)), (sums, sp.lead("second", 8, dh))],
        [(sds((H, d, 3 * dh), BF16), sp.lead("second", d, 3 * dh)), whole(sds((n, d), F32)), whole(sds((HALO, d), F32)),
         whole(sds((H, 72, dh), F32))],
        [pltpu.VMEM((H, n, dh), BF16), pltpu.VMEM((H, n, dh), BF16), pltpu.VMEM((H, n, dh), BF16),
         pltpu.VMEM((n, 128), BF16), pltpu.VMEM((8, 128), F32),
         pltpu.VMEM((dh + 128, dh), BF16), pltpu.VMEM((dh + 128, dh), BF16), pltpu.VMEM((n, 128), F32),
         pltpu.VMEM((128, n), F32), pltpu.VMEM((8, 128), F32),
         pltpu.VMEM((HALO, d), F32), pltpu.VMEM((n + 2 * HALO, dh), F32), pltpu.VMEM((n + HALO, dh), F32),
         pltpu.VMEM((n, 2 * dh), BF16), pltpu.VMEM((n, dh), BF16), pltpu.VMEM((dh // 128, 128, 256), BF16), pltpu.VMEM((dh // 128, 128, 128), BF16),
         pltpu.VMEM((3, 128, dh), BF16), state, state, sem, sem],
        collective_id=3, has_side_effects=True,
    )

    total, minor, corr = scattered(grads, minor, corr)
    rows = total.shape[0]
    once = lambda *shape: pl.BlockSpec(shape, lambda i: (0,) * len(shape))
    tail = pl.BlockSpec((HALO, d), lambda i: (n // HALO - 1, 0))
    lines = (dh // 128, 128)
    shapes = [(rows, 2, dh), (rows, dh), (TAPS, dh), lines, (3, 4, 4, dh // 4), (3, 2 * H, dh), (1, 2), lines, lines,
              (d // 128, 128)]
    anywhere = pl.BlockSpec(memory_space=pl.ANY)
    up, down, conv_w, conv_b, maps, gate_w, gate_b, group, skip, gain, ing, output = pl.pallas_call(
        partial(finish_kernel, H),
        grid=(1,),
        out_shape=[*(sds(shape, F32) for shape in shapes), sds((n, d), F32), sds((n, d), BF16)],
        in_specs=[once(*total.shape), once(*minor.shape), once(*corr.shape), tail, anywhere],
        out_specs=[*(once(*shape) for shape in shapes), tail, anywhere],
        input_output_aliases={3: 10, 4: 11},
        name="finish",
    )(total, minor, corr, ing, output)
    return (output, ing, gain.reshape(d), up, conv_w, conv_b.reshape(dh), maps.transpose(0, 3, 1, 2),
            gate_w.transpose(0, 2, 1), gate_b.T, group.reshape(dh), skip.reshape(dh), down.T)


def solution(mesh):
    rows = P(("dp", "head"), None)
    small = (P(None, "head"), P("head"), P(None, "head", None, None), P(None, "head", None), P(None, "head"))
    return jax.shard_map(
        local,
        mesh=mesh,
        in_specs=(rows, P("dp"), P(), P("dp", None, "head"), *small, P("head"), P("head"), P("head", "dp"), rows),
        out_specs=(rows, rows, P(), P("dp", None, "head"), *small, P("head"), P("head"), P("head", "dp")),
        check_vma=False,
    )
```

profile of v0, /device:TPU:0, one launch (start us, length us, event | category | flops | bytes accessed | tf_op | source)
XLA Modules:
  0.0 257.9 jit_solution(4565586410526177799)
XLA Ops:
  0.6 45.3 %gather.1 = (bf16[4,768,1152]{2,1,0:T(8,128)(2,1)}, f32[4,48,384]{2,1,0:T(8,128)}, bf16[16,768]{1,0:T(8,128)(2,1)}) custom-call(bf16[96,2,384]{2,1,0:T(2,128)(2,1)} %up_raw.1, bf16[96,384]{1,0:T(8,128)(2,1)} %bitcast.17, f32[4,384]{1,0:T(4,128)} %taps.1, f32[3,128]{1,0:T(4,128)} %bitcast.23, f32[3,128]{1,0:T(4,128)} %bitcast.24, f32[3,128]{1,0:T(4,128)} %bitcast.25, ...), custom_call_target="tpu_custom_call" | custom-call | tf_op jit(solution)/shard_map/gather/pallas_call | solution.py:839
  46.0 23.2 %lift.1 = (bf16[4,1024,384]{2,1,0:T(8,128)(2,1)}, bf16[4,1024,384]{2,1,0:T(8,128)(2,1)}, bf16[4,1024,512]{2,1,0:T(8,128)(2,1)}, bf16[4,1024,384]{2,1,0:T(8,128)(...) custom-call(bf16[1024,768]{1,0:T(8,128)(2,1)} %x_ref.5, ...), custom_call_target="tpu_custom_call" | custom-call | tf_op jit(solution)/shard_map/lift/pallas_call | solution.py:1074
  69.1 47.9 %forward.1 = (bf16[1024,768]{1,0:T(8,128)(2,1)}, f32[1024,128]{1,0:T(8,128)}, f32[8,1024]{1,0:T(8,128)}, f32[4,8,128]{2,1,0:T(8,128)}, bf16[4,768,384]{2,1,0:T(8...) custom-call(bf16[1024,768]{1,0:T(8,128)(2,1)} %x_ref.5, ...), custom_call_target="tpu_custom_call" | custom-call | tf_op jit(solution)/shard_map/forward/pallas_call | solution.py:1074
  117.1 84.2 %backward.1 = (bf16[4,768,1152]{2,1,0:T(8,128)(2,1)}, f32[1024,768]{1,0:T(8,128)}, f32[16,768]{1,0:T(8,128)}, f32[4,72,384]{2,1,0:T(8,128)}) custom-call(bf16[1024,768]{1,0:T(8,128)(2,1)} %x_ref.5, bf16[16,768]{1,0:T(8,128)(2,1)} %get-tuple-element.55.halo_ref, f32[6,128]{1,0:T(8,128)} %bitcast.22, f32[16,128]{1,0:T(8,128)} %get-tuple-element.58.flags_ref, ...), custom_call_target="tpu_custom_call" | custom-call | tf_op jit(solution)/shard_map/backward/pallas_call | solution.py:1074
  201.3 49.4 %scatter.1 = (f32[96,1152]{1,0:T(8,128)}, f32[72,384]{1,0:T(8,128)}, f32[16,768]{1,0:T(8,128)}) custom-call(bf16[4,768,1152]{2,1,0:T(8,128)(2,1)} %get-tuple-element.78.part, f32[4,72,384]{2,1,0:T(8,128)} %get-tuple-element.79.minor, f32[16,768]{1,0:T(8,128)} %get-tuple-element.80.corr), custom_call_target="tpu_custom_call" | custom-call | tf_op jit(solution)/shard_map/scatter/pallas_call | solution.py:976
  250.7 2.5 finish.1
  253.2 0.0 copy-start
  253.2 2.8 %copy.31 = bf16[1024,768]{1,0:T(8,128)(2,1)} copy(bf16[1024,768]{1,0:T(8,128)(2,1)} %get-tuple-element.110) | data formatting | bytes 3145728
  256.0 0.0 copy-done
  256.0 1.7 copy.32
Async XLA Ops:
  253.2 2.8 %copy-start = (f32[1024,768]{1,0:T(8,128)S(1)}, f32[1024,768]{1,0:T(8,128)}, u32[]{:S(2)}) copy-start(f32[1024,768]{1,0:T(8,128)} %get-tuple-element.111) | copy-start | bytes 9437188
where the time goes:
time: 260 us; the launch traced here: 258 us
  Pallas kernels  252 us (97%)
  local copies, waits for them, and re-layouts  4.47 us (2%)
    pallas_call x3, Pallas kernels, call(): pl.pallas_call(kernel, grid=(H * rounds,), out_shape=[o[0] for o in outs]...  155 us
    pallas_call x1, Pallas kernels, scattered(): pl.pallas_call(scatter_kernel, out_shape=[sds((rows, cols), F32), sds(lin...  49.4 us
    pallas_call x1, Pallas kernels, gathered(): pl.pallas_call(gather_kernel, out_shape=[sds((heads, dp * rows, 3 * dh),...  45.3 us

commit v1 on v0

--- a/solution.py
+++ b/solution.py
@@ -206,11 +206,14 @@
 def forward_kernel(n_heads, log_scale,
                    x_ref, og_all_ref, gates_ref, flags_ref, q_ref, k_ref, va_ref, gate_ref, pre_ref, pack_ref, w_ref,
                    out_ref, gcol_ref, grow_ref, retain_ref, dng_ref, sttot_ref, gloc_ref, gend_ref, gaug_ref, ogg_ref,
-                   dskip_ref, sums_ref,
-                   acc, ogt, numer, mixed_s, stb, gt, gn, sloc, leaving, landed, retain, ss, rs):
+                   dskip_ref, sums_ref, gin_ref,
+                   acc, ogt, numer, mixed_s, stb, gt, gn, sloc, leaving, landed, retain, ss, rs,
+                   back_leaving, back_landed, back_ss, back_rs):
     step = pl.program_id(0)
     chain = Chain(1, retain, flags_ref[0:1, 0:1], leaving, landed, (ss, rs))
     place = chain.place
+    early = range(back_landed.shape[0])
+    back = Chain(-1, retain, flags_ref[8:9, 0:1], back_leaving, back_landed, (back_ss, back_rs), early)
 
     @pl.when(step == 0)
     def _():
@@ -254,10 +257,24 @@
             out_ref, dng_ref, sttot_ref, gloc_ref, gend_ref, gaug_ref, ogg_ref, dskip_ref, sums_ref,
             acc, ogt, numer, mixed_s, stb, gt, gn)
 
+        for i in early:
+
+            @pl.when(h == i)
+            def _():
+                back_leaving[i] = gend_ref[0]
+
+        for i in early:
+
+            @pl.when(h == jnp.minimum(back.place + i, n_heads - 1))
+            def _():
+                back.pump(i)
+
     @pl.when(step == 2 * n_heads - 1)
     def _():
         retain_ref[...] = retain[...]
+        gin_ref[...] = back_landed[...]
         chain.finish()
+        back.finish()
 
 
 def mix(h, n_heads, log_scale,
@@ -381,10 +398,10 @@
 
     @pl.when((chain.place == 1) & (h == 0))
     def _():
-        for i in range(1, n_heads):
+        for i in chain.carried:
             chain.pump(i)
 
-    @pl.when(chain.place > 1)
+    @pl.when((chain.place > 2) & (h >= chain.carried[0]))
     def _():
         chain.pump(h)
 
@@ -437,23 +454,24 @@
 
 
 def lower(h, n_heads,
-          x_ref, halo_ref, gain_ref, flags_ref, og_all_ref, normt_ref, pg_ref, bsum_ref, q_ref, k_ref, va_ref,
+          halo_ref, gain_ref, flags_ref, normt_ref, pg_ref, bsum_ref, q_ref, k_ref, va_ref,
           dq_s, dk_s, dv_s, pre_ref, br_ref, ogg_ref, dskip_ref,
-          pack_ref, w_ref, dng_ref, sums_ref,
-          upg_ref, ing_ref, corr_ref, minor_ref,
-          nacc, pext, brx, lifted, conv_s, wqk, wv, gw):
+          pack_ref, w_ref, sums_ref,
+          upg_ref, ng_ref, corr_ref, minor_ref,
+          pext, lifted, conv_s, wqk, wv, gw, gacc, first, last):
     n, dh = q_ref.shape
     link = flags_ref[0:1, 0:1]
     w = w_ref.at[0]
 
     minor_out = minor_ref
     minor_ref = minor_out.at[pl.ds(h, 1)]
-    minor_ref[0, 64:] = jnp.zeros((minor_ref.shape[1] - 64, dh), F32)
-
-    @pl.when(h == 0)
-    def _():
-        nacc[...] = jnp.zeros_like(nacc)
-        ing_ref[...] = jnp.zeros_like(ing_ref)
+    minor_ref[0, 67:] = jnp.zeros((minor_ref.shape[1] - 67, dh), F32)
+
+    @pl.when(first)
+    def _():
+        corr_ref[...] = jnp.zeros_like(corr_ref)
+        ng_ref[...] = jnp.zeros_like(ng_ref)
+        gacc[...] = jnp.zeros_like(gacc)
         pext[0:HALO] = jnp.zeros((HALO, dh), F32)
         pext[HALO + n :] = jnp.zeros((HALO, dh), F32)
         gw[...] = jnp.zeros_like(gw)
@@ -464,9 +482,6 @@
         wqk[b, :, 0:128] = q_high
         wqk[b, :, 128:256] = k_high
         wv[b] = v_high
-
-    for r, rows in row_chunks(n + HALO, 208):
-        brx[r : r + rows] = br_ref[r : r + rows].astype(F32)
 
     taps = [jnp.zeros((1, dh), F32) for _ in range(TAPS)]
     bias_sum = jnp.zeros((1, dh), F32)
@@ -490,22 +505,20 @@
             pext[HALO + r : HALO + r + rows, at] = conv_grad * slope[:, at]
         pre_grad = pext[HALO + r : HALO + r + rows]
         bias_sum = bias_sum + jnp.sum(pre_grad, axis=0, keepdims=True)
+        branch = br_ref[r : r + rows + HALO].astype(F32)
         for j in range(TAPS):
-            taps[j] = taps[j] + jnp.sum(
-                pre_grad * brx[HALO + r - j : HALO + r - j + rows], axis=0, keepdims=True
-            )
+            taps[j] = taps[j] + jnp.sum(pre_grad * branch[HALO - j : HALO - j + rows], axis=0, keepdims=True)
     for j in range(TAPS):
         minor_ref[0, j : j + 1] = taps[j]
     minor_ref[0, TAPS : TAPS + 1] = bias_sum
     minor_ref[0, TAPS + 1 : 8] = jnp.zeros((8 - TAPS - 1, dh), F32)
     minor_ref[0, 8:16] = sums_ref[0]
-    upg_ref[0, :, 2 * dh : 3 * dh] = dng_ref[0]
 
     halo_grad = jnp.zeros((HALO, dh), F32)
     for j in range(1, TAPS):
         halo_grad = halo_grad + pack_ref[0, j : j + 1] * pext[j : HALO + j]
     halo_b = (halo_grad * link).astype(BF16)
-    nacc[0:HALO] += nt(halo_b, w[:, 0:dh])
+    corr_ref[...] += nt(halo_b, w[:, 0:dh])
     for r, rows in row_chunks(n, CH):
         span = slice(r, r + rows)
         grad = jnp.zeros((rows, dh), F32)
@@ -515,90 +528,307 @@
             at = slice(128 * b, 128 * b + 128)
             lifted[span, at] = (grad[:, at] + nt(dv_s[h, span, at], wv[b])).astype(BF16)
         lifted[span, dh : 2 * dh] = ogg_ref[span]
-        ing_ref[span] += nt(lifted[span], w[...])
-
-    unit_halo, std_halo = normalised(halo_ref[...].astype(F32))
+        ng_ref[span] += nt(lifted[span], w[...])
+
+    unit_halo, _ = normalised(halo_ref[...].astype(F32))
     gain = jnp.concatenate([gain_ref[j : j + 1] for j in range(gain_ref.shape[0])], axis=1)
-    upg = nn(normt_ref[...], lifted[...])
-    upg_ref[0, :, dh : 2 * dh] = upg[:, dh:].astype(BF16)
-    upg_ref[0, :, 0:dh] = (upg[:, 0:dh] + tn((unit_halo * gain).astype(BF16), halo_b)).astype(BF16)
+    normed_halo = (unit_halo * gain).astype(BF16)
+    d = normt_ref.shape[0]
+    for r, rows in row_chunks(d, d // 2):
+        span = slice(r, r + rows)
+        upg = nn(normt_ref[span], lifted[...])
+        upg = jnp.concatenate([upg[:, 0:dh] + tn(normed_halo[:, span], halo_b), upg[:, dh:]], axis=1)
+        upg_ref[span] = upg.astype(BF16)
+        along = upg * w[span].astype(F32)
+        part = along[:, 0:128]
+        for at in range(128, 2 * dh, 128):
+            part = part + along[:, at : at + 128]
+        gacc[span] += part
 
     fold = jnp.where(iota((8, 128), 1) % 4 == iota((8, 128), 0), 1.0, 0.0)
     diagonal = iota((128, 128), 0) // 4 == iota((128, 128), 1) // 4
     for b in range(dh // 128):
         at = slice(128 * b, 128 * b + 128)
         qk_grad = tn(conv_s[:, at], jnp.concatenate([dq_s[h, :, at], dk_s[h, :, at]], axis=1))
-        v_grad = tn(brx[HALO:, at].astype(BF16), dv_s[h, :, at])
+        v_grad = tn(br_ref[HALO:, at], dv_s[h, :, at])
         for m, full in enumerate((qk_grad[:, 0:128], qk_grad[:, 128:256], v_grad)):
             minor_ref[0, 16 + 8 * m : 24 + 8 * m, at] = nt(fold, jnp.where(diagonal, full, 0.0), precision=HIGHEST)
     minor_ref[0, 40:48] = tn(pg_ref[...], q_ref[...])[0:8]
     minor_ref[0, 48:56] = tn(pg_ref[...], k_ref[...])[0:8]
     minor_ref[0, 56:64] = tn(pg_ref[...], va_ref[0, :, 0:dh])[0:8]
 
-    @pl.when(h == n_heads - 1)
-    def _():
-        def back(normed_grad, unit, inv_std):
-            scaled = normed_grad * gain
-            return inv_std * (
-                scaled
-                - jnp.mean(scaled, axis=1, keepdims=True)
-                - unit * jnp.mean(scaled * unit, axis=1, keepdims=True)
-            )
-
-        corr_ref[...] = back(nacc[0:HALO], unit_halo, std_halo)
-        total = jnp.sum(nacc[0:HALO] * unit_halo, axis=0, keepdims=True)
-        for r, rows in row_chunks(n, CH):
-            unit, inv_std = normalised(x_ref[r : r + rows].astype(F32))
-            grads = ing_ref[r : r + rows]
-            total = total + jnp.sum(grads * unit, axis=0, keepdims=True)
-            ing_ref[r : r + rows] = og_all_ref[r : r + rows].astype(F32) + back(grads, unit, inv_std)
+    @pl.when(last)
+    def _():
+        total = nt(jnp.ones((8, 128), F32), gacc[...], precision=HIGHEST)[0:1] / gain
         for i in range(n_heads):
             minor_out[i, 66:67] = jnp.broadcast_to(bsum_ref[0:1, n_heads + i : n_heads + i + 1], (1, dh))
-            for j in range(total.shape[1] // dh):
+            for j in range(d // dh):
                 minor_out[i, 64 + j : 65 + j] = total[:, dh * j : dh * j + dh]
 
 
-def backward_kernel(n_heads, log_scale,
-                    x_ref, halo_ref, gain_ref, flags_ref, og_all_ref, normt_ref, gates_ref, gcol_ref, grow_ref, retain_ref,
-                    gend_ref, q_ref, k_ref, va_ref, gaug_ref, sttot_ref, gloc_ref, pre_ref, br_ref, ogg_ref, dskip_ref,
-                    pack_ref, w_ref, dng_ref, sums_ref,
-                    upg_ref, ing_ref, corr_ref, minor_ref,
-                    dq_s, dk_s, dv_s, pg_s, bsum, stb, gtb, cols, rowsb, across,
-                    nacc, pext, brx, lifted, conv_s, wqk, wv, gw, leaving, landed, ss, rs):
+def backward_kernel(inside, n_heads, log_scale,
+                    halo_ref, gain_ref, flags_ref, normt_ref, gates_ref, gcol_ref, grow_ref, retain_ref,
+                    gend_ref, gin_ref, q_ref, k_ref, va_ref, gaug_ref, sttot_ref, gloc_ref, pre_ref, br_ref, ogg_ref,
+                    dskip_ref, pack_ref, w_ref, sums_ref, *rest):
+    if inside:
+        dng, up_total, down_total, minor_total, corr_in, ng_ref, *rest = rest
+    else:
+        upg_ref, minor_ref, corr_ref, ng_ref, *rest = rest
+    (dq_s, dk_s, dv_s, pg_s, bsum, stb, gtb, cols, rowsb, across, pext, lifted, conv_s, wqk, wv, gw, gacc,
+     leaving, landed, ss, rs, *rest) = rest
     step = pl.program_id(0)
-    chain = Chain(-1, retain_ref, flags_ref[8:9, 0:1], leaving, landed, (ss, rs))
+    done = gin_ref.shape[0]
+    chain = Chain(-1, retain_ref, flags_ref[8:9, 0:1], leaving, landed, (ss, rs), range(done, n_heads))
+    dh = q_ref.shape[1]
+    near_k, near_v = ng_ref.at[:, 0:dh], ng_ref.at[:, dh : 2 * dh]
+    if inside:
+        here = Place()
+        upg_ref, minor_ref, corr_ref, landing, m0, m1, n0, n1, load, ms, mr, *rest = rest
+        many = len(rest) // 2
+        up = Scatter(here, *rest[:many])
+        down = Scatter(here, *rest[many:])
 
     @pl.when(step == 0)
     def _():
-        chain.greet()
+        if inside:
+            greet([here.device(**to) for to in NEIGHBOURS])
+        else:
+            chain.greet()
         leaving[...] = gend_ref[...]
+        landed[0:done] = gin_ref[...]
 
         @pl.when(chain.place == 0)
         def _():
-            for i in range(n_heads):
+            for i in chain.carried:
                 chain.pump(i)
 
-        @pl.when(chain.place == 1)
-        def _():
-            chain.pump(0)
-
-    dh = q_ref.shape[1]
-    near_k, near_v = ing_ref.at[:, 0:dh], ing_ref.at[:, dh : 2 * dh]
+    @pl.when((step >= done) & (step < n_heads) & (chain.place == 2))
+    def _():
+        chain.pump(step)
 
     @pl.when(step < n_heads)
     def _():
         memory_back(step, n_heads, log_scale, chain, gates_ref, gcol_ref, grow_ref, q_ref, k_ref, va_ref, gaug_ref,
                     sttot_ref, gloc_ref, dq_s, dk_s, dv_s, pg_s, bsum, near_k, near_v, stb, gtb, cols, rowsb, across)
 
+    if inside:
+
+        @pl.when(step == n_heads + 1)
+        def _():
+            up.given(1)
+
+        @pl.when(step == n_heads + 3)
+        def _():
+            up.given(0)
+
     @pl.when(step >= n_heads)
     def _():
-        lower(step - n_heads, n_heads, x_ref, halo_ref, gain_ref, flags_ref, og_all_ref, normt_ref, pg_s, bsum, q_ref,
-              k_ref, va_ref, dq_s, dk_s, dv_s, pre_ref, br_ref, ogg_ref, dskip_ref, pack_ref, w_ref, dng_ref, sums_ref,
-              upg_ref, ing_ref, corr_ref, minor_ref, nacc, pext, brx, lifted, conv_s, wqk, wv, gw)
+        i = step - n_heads
+        lower(turned(i), n_heads, halo_ref, gain_ref, flags_ref, normt_ref, pg_s, bsum, q_ref,
+              k_ref, va_ref, dq_s, dk_s, dv_s, pre_ref, br_ref, ogg_ref, dskip_ref, pack_ref, w_ref, sums_ref,
+              upg_ref, ng_ref, corr_ref, minor_ref, pext, lifted, conv_s, wqk, wv, gw, gacc, i == 0, i == n_heads - 1)
+
+    if inside:
+        loads = [pltpu.make_async_copy(dng.at[here.head(fx, 0)], down.own.at[fx], load.at[fx]) for fx in (0, 1)]
+
+        def at_end_of(number):
+            return pl.when(step == number)
+
+        @at_end_of(1)
+        def _():
+            for fx in (1, 0):
+                loads[fx].start()
+                down.give(dng.at[here.head(fx, 1)], fx)
+
+        @at_end_of(2)
+        def _():
+            for fx in (1, 0):
+                loads[fx].wait()
+                for k in ORDER:
+                    down.first(fx, k)
+
+        @at_end_of(3)
+        def _():
+            for k in ORDER:
+                down.away(k)
+
+        @at_end_of(4)
+        def _():
+            up.give(upg_ref, 1)
+            for k in ORDER:
+                down.home(k)
+
+        @at_end_of(5)
+        def _():
+            up.own[1] = upg_ref[...]
+            for k in ORDER:
+                up.first(1, k)
+            for k in ORDER:
+                down.third(k)
+
+        @at_end_of(6)
+        def _():
+            up.give(upg_ref, 0)
+            for k in ORDER:
+                up.away(k)
+            down.final(down_total)
+
+        @at_end_of(7)
+        def _():
+            up.own[0] = upg_ref[...]
+            before = (here.z * 2 + here.y, lax.rem(here.head() + 3, 4))
+            sent = [remote(corr_ref, landing, (ms, mr), 6, before)]
+            sent[0].start()
+
+            def send(src, dst, at, to):
+                copy = remote(src, dst, (ms, mr), at, here.device(**to))
+                copy.start()
+                sent.append(copy)
+
+            def arrived(dst, at):
+                remote(dst, dst, (ms, mr), at, here.device(fc=1)).wait_recv()
+
+            for fx in (0, 1):
+                send(minor_ref.at[here.head(fx, 1)], n0.at[fx], fx, dict(fc=1))
+            up.first(0, 1)
+            up.first(0, 2)
+            for fx in (1, 0):
+                arrived(n0.at[fx], fx)
+                m0[fx] = minor_ref[here.head(fx, 0)] + n0[fx]
+            send(m0.at[1], n1.at[0], 2, dict(fx=1))
+            up.home(1)
+            up.first(0, 3)
+            up.first(0, 0)
+            up.home(2)
+            arrived(n1.at[0], 2)
+            m1[0] = m0[0] + n1[0]
+            send(m1.at[0], n1.at[1], 3, dict(fy=1))
+            up.third(1)
+            up.home(3)
+            up.third(2)
+            arrived(n1.at[1], 3)
+            m1[1] = m1[0] + n1[1]
+            send(m1.at[1], n1.at[2], 4, dict(k=1))
+            up.home(0)
+            up.third(3)
+            arrived(n1.at[2], 4)
+            m1[2] = m1[1] + n1[2]
+            send(m1.at[2], n1.at[3], 5, dict(k=2))
+            up.third(0)
+            up.final(up_total)
+            arrived(n1.at[3], 5)
+            minor_total[...] = m1[2] + n1[3]
+            arrived(landing, 6)
+            corr_in[...] = landing[...]
+            for copy in sent:
+                copy.wait_send()
+            down.given(1)
+            down.given(0)
+            up.finish()
+            down.finish()
 
     @pl.when(step == 2 * n_heads - 1)
     def _():
         chain.finish()
+
+
+ORDER = (1, 2, 3, 0)
+
+
+class Scatter:
+    SEMAPHORES = ((2, 4), (2, 4), (2, 2, 4), (2, 2, 4), (2, 4), (2, 4), (2, 3), (2, 3))
+
+    @staticmethod
+    def scratch(d, rows, cols):
+        half = rows // 2
+        sem = pltpu.SemaphoreType.DMA
+        return [pltpu.VMEM((2, d, cols), BF16), pltpu.VMEM((2, d, cols), BF16), pltpu.VMEM((2, 4, half, cols), BF16),
+                pltpu.VMEM((2, 4, half, cols), BF16), pltpu.VMEM((2, 4, half, cols), BF16),
+                pltpu.VMEM((2, 3, half, cols), BF16), *(sem(shape) for shape in Scatter.SEMAPHORES)]
+
+    def __init__(self, here, own, r0, r1a, r1b, r2, r3, *sems):
+        self.here, self.own, self.r0, self.r1a, self.r1b, self.r2, self.r3 = here, own, r0, r1a, r1b, r2, r3
+        self.s0, self.s1, self.s2, self.s3 = (tuple(sems[i : i + 2]) for i in (0, 2, 4, 6))
+        self.half = r3.shape[2]
+
+    def piece(self, fx, k, fy, p):
+        return self.own.at[fx, pl.ds(self.here.rows(k, fy, 2 * self.half) + self.half * p, self.half)]
+
+    def pair(self, k):
+        return pl.ds(pl.multiple_of(self.here.along_z(k) * 4 * self.half, 16), 4 * self.half)
+
+    def send(self, src, dst, sems, at, to):
+        remote(src, dst, sems, at, self.here.device(**to)).start()
+
+    def arrived(self, dst, sems, at):
+        remote(dst, dst, sems, at, self.here.device(fc=1)).wait_recv()
+
+    def sent(self, src, sems, at):
+        remote(src, src, sems, at, self.here.device(fc=1)).wait_send()
+
+    def add(self, into, other):
+        into[...] = (into[...].astype(F32) + other[...].astype(F32)).astype(BF16)
+
+    def give(self, src, fx):
+        for k in ORDER:
+            self.send(src.at[self.pair(k)], self.r0.at[fx, self.pair(k)], self.s0, (fx, k), dict(fc=1))
+
+    def given(self, fx):
+        for k in range(4):
+            self.sent(self.r0.at[fx, self.pair(k)], self.s0, (fx, k))
+
+    def first(self, fx, k):
+        self.arrived(self.r0.at[fx, self.pair(k)], self.s0, (fx, k))
+        self.add(self.own.at[fx, self.pair(k)], self.r0.at[fx, self.pair(k)])
+        self.send(self.piece(fx, k, 1, 0), self.r1a.at[fx, k], self.s1, (0, fx, k), dict(fy=1))
+        if fx:
+            for fy in (1, 0):
+                self.send(self.piece(1, k, fy, 1), self.r1b.at[fy, k], self.s1, (1, fy, k), dict(fx=1))
+
+    def away(self, k):
+        self.arrived(self.r1a.at[1, k], self.s1, (0, 1, k))
+        self.add(self.piece(1, k, 0, 0), self.r1a.at[1, k])
+        self.send(self.piece(1, k, 0, 0), self.r2.at[0, k], self.s2, (0, k), dict(fx=1))
+
+    def home(self, k):
+        self.arrived(self.r1a.at[0, k], self.s1, (0, 0, k))
+        self.add(self.piece(0, k, 0, 0), self.r1a.at[0, k])
+        for f in (1, 0):
+            self.arrived(self.r1b.at[f, k], self.s1, (1, f, k))
+            self.add(self.piece(0, k, f, 1), self.r1b.at[f, k])
+            if f:
+                self.send(self.piece(0, k, 1, 1), self.r2.at[1, k], self.s2, (1, k), dict(fy=1))
+
+    def third(self, k):
+        for p in (0, 1):
+            self.arrived(self.r2.at[p, k], self.s2, (p, k))
+            self.add(self.piece(0, k, 0, p), self.r2.at[p, k])
+            if k:
+                self.send(self.piece(0, k, 0, p), self.r3.at[p, k - 1], self.s3, (p, k - 1), dict(k=k))
+
+    def final(self, total):
+        for p in (0, 1):
+            summed = self.piece(0, 0, 0, p)[...].astype(F32)
+            for k in range(3):
+                self.arrived(self.r3.at[p, k], self.s3, (p, k))
+                summed = summed + self.r3[p, k].astype(F32)
+            total[self.half * p : self.half * p + self.half] = summed
+
+    def finish(self):
+        for k in range(4):
+            for f in (0, 1):
+                self.sent(self.r1a.at[f, k], self.s1, (0, f, k))
+                self.sent(self.r1b.at[f, k], self.s1, (1, f, k))
+                self.sent(self.r2.at[f, k], self.s2, (f, k))
+                if k < 3:
+                    self.sent(self.r3.at[f, k], self.s3, (f, k))
+
+
+def turned(i):
+    head = lax.axis_index("head")
+    x, c = lax.div(head, 2), lax.rem(head, 2)
+    fx, fc = 1 - lax.div(i, 2), 1 - lax.rem(i, 2)
+    return (x + fx - 2 * x * fx) * 2 + (c + fc - 2 * c * fc)
 
 
 class Specs:
@@ -608,6 +838,8 @@
             both=lambda s: lax.rem(s, heads),
             first=lambda s: jnp.minimum(s, heads - 1),
             second=lambda s: jnp.maximum(s - heads, 0),
+            turned=lambda s: turned(jnp.maximum(s - heads, 0)),
+            mixed=lambda s: jnp.where(s < heads, s, turned(jnp.maximum(s - heads, 0))),
         )
 
     def whole(self, *shape):
@@ -852,151 +1084,29 @@
     return lax.axis_size("dp") == 8 and lax.axis_size("head") == 4 and rows % 32 == 0
 
 
-def scatter_kernel(part, minor, corr, total, minor_total, corr_in,
-                   own, r0, r1a, r1b, r2, r3, m0, m1, n0, n1,
-                   load, s0, t0, s1, t1, s2, t2, s3, t3, ms, mr):
-    here = Place()
-    rows = total.shape[0]
-    half = rows // 2
-    spans = (pl.ds(0, half), pl.ds(half, half))
-    order = (1, 2, 3, 0)
-    corners = ((1, 1), (1, 0), (0, 1), (0, 0))
-
-    def block(k, fx, fy, fc):
-        return part.at[here.head(fx, fc), pl.ds(here.rows(k, fy, rows), rows)]
-
-    loads = {}
-    for k in order:
-        for fx, fy in corners:
-            loads[k, fx, fy] = pltpu.make_async_copy(block(k, fx, fy, 0), own.at[fx, k, fy], load.at[fx, k, fy])
-            loads[k, fx, fy].start()
-    small = [pltpu.make_async_copy(minor.at[here.head(fx)], m0.at[fx], load.at[fx, 4, 0]) for fx in (0, 1)]
-    for copy in small:
-        copy.start()
-    greet([here.device(**to) for to in NEIGHBOURS])
-    started = []
-
-    def send(src, dst, sems, at, to):
-        copy = remote(src, dst, sems, at, to if isinstance(to, tuple) else here.device(**to))
-        copy.start()
-        started.append(copy)
-
-    def arrived(dst, sems, at):
-        remote(dst, dst, sems, at, here.device(fc=1)).wait_recv()
-
-    def add(into, other):
-        into[...] = (into[...].astype(F32) + other[...].astype(F32)).astype(into.dtype)
-
-    def first(k):
-        for fx, fy in corners:
-            loads[k, fx, fy].wait()
-            arrived(r0.at[fx, k, fy], (s0, t0), (fx, k, fy))
-            add(own.at[fx, k, fy], r0.at[fx, k, fy])
-            if fy:
-                send(own.at[fx, k, 1, spans[0]], r1a.at[fx, k], (s1, t1), (0, fx, k), dict(fy=1))
-            if fx:
-                send(own.at[1, k, fy, spans[1]], r1b.at[fy, k], (s1, t1), (1, fy, k), dict(fx=1))
-
-    def second(k):
-        for f in (1, 0):
-            arrived(r1a.at[f, k], (s1, t1), (0, f, k))
-            add(own.at[f, k, 0, spans[0]], r1a.at[f, k])
-            if f:
-                send(own.at[1, k, 0, spans[0]], r2.at[0, k], (s2, t2), (0, k), dict(fx=1))
-            arrived(r1b.at[f, k], (s1, t1), (1, f, k))
-            add(own.at[0, k, f, spans[1]], r1b.at[f, k])
-            if f:
-                send(own.at[0, k, 1, spans[1]], r2.at[1, k], (s2, t2), (1, k), dict(fy=1))
-
-    def third(k):
-        for p in (0, 1):
-            arrived(r2.at[p, k], (s2, t2), (p, k))
-            add(own.at[0, k, 0, spans[p]], r2.at[p, k])
-            if k:
-                send(own.at[0, k, 0, spans[p]], r3.at[p, k - 1], (s3, t3), (p, k - 1), dict(k=k))
-
-    send(corr, corr_in, (ms, mr), 6, (here.z * 2 + here.y, lax.rem(here.head() + 3, 4)))
-    for fx in (0, 1):
-        send(minor.at[here.head(fx, 1)], n0.at[fx], (ms, mr), fx, dict(fc=1))
-    for k in order:
-        for fx, fy in corners:
-            send(block(k, fx, fy, 1), r0.at[fx, k, fy], (s0, t0), (fx, k, fy), dict(fc=1))
-    for fx in (0, 1):
-        small[fx].wait()
-        arrived(n0.at[fx], (ms, mr), fx)
-        add(m0.at[fx], n0.at[fx])
-    send(m0.at[1], n1.at[0], (ms, mr), 2, dict(fx=1))
-    first(1)
-    first(2)
-    second(1)
-    arrived(n1.at[0], (ms, mr), 2)
-    m1[0] = m0[0] + n1[0]
-    send(m1.at[0], n1.at[1], (ms, mr), 3, dict(fy=1))
-    first(3)
-    second(2)
-    third(1)
-    arrived(n1.at[1], (ms, mr), 3)
-    m1[1] = m1[0] + n1[1]
-    send(m1.at[1], n1.at[2], (ms, mr), 4, dict(k=1))
-    first(0)
-    second(3)
-    third(2)
-    arrived(n1.at[2], (ms, mr), 4)
-    m1[2] = m1[1] + n1[2]
-    send(m1.at[2], n1.at[3], (ms, mr), 5, dict(k=2))
-    second(0)
-    third(3)
-    third(0)
-    for p in (0, 1):
-        summed = own[0, 0, 0, spans[p]].astype(F32)
-        for k in range(3):
-            arrived(r3.at[p, k], (s3, t3), (p, k))
-            summed = summed + r3[p, k].astype(F32)
-        total[spans[p]] = summed
-    arrived(n1.at[3], (ms, mr), 5)
-    minor_total[...] = m1[2] + n1[3]
-    arrived(corr_in, (ms, mr), 6)
-    for copy in started:
-        copy.wait_send()
-
-
-def scattered(part, minor, corr):
-    dp = lax.axis_size("dp")
-    heads, d, cols = part.shape
-    rows = d // dp
-    if not by_hand(rows):
-        part = lax.psum_scatter(part, "head", scatter_dimension=0, tiled=True)
-        part = lax.psum_scatter(part, "dp", scatter_dimension=1, tiled=True)[0].astype(F32)
-        minor = lax.psum(lax.psum_scatter(minor, "head", scatter_dimension=0, tiled=True), "dp")[0]
-        return part, minor, shifted(corr, -1)
-    sem = pltpu.SemaphoreType.DMA
-    half = rows // 2
-    lines = minor.shape[1:]
-    vmem = pl.BlockSpec(memory_space=pltpu.VMEM)
-    return pl.pallas_call(
-        scatter_kernel,
-        out_shape=[sds((rows, cols), F32), sds(lines, F32), sds(corr.shape, F32)],
-        in_specs=[pl.BlockSpec(memory_space=pl.ANY)] * 3,
-        out_specs=[vmem] * 3,
-        scratch_shapes=[
-            pltpu.VMEM((2, 4, 2, rows, cols), BF16), pltpu.VMEM((2, 4, 2, rows, cols), BF16),
-            pltpu.VMEM((2, 4, half, cols), BF16), pltpu.VMEM((2, 4, half, cols), BF16),
-            pltpu.VMEM((2, 4, half, cols), BF16), pltpu.VMEM((2, 3, half, cols), BF16),
-            pltpu.VMEM((2, *lines), F32), pltpu.VMEM((3, *lines), F32),
-            pltpu.VMEM((2, *lines), F32), pltpu.VMEM((4, *lines), F32),
-            sem((2, 5, 2)), sem((2, 4, 2)), sem((2, 4, 2)), sem((2, 2, 4)), sem((2, 2, 4)), sem((2, 4)), sem((2, 4)),
-            sem((2, 3)), sem((2, 3)), sem((7,)), sem((7,)),
-        ],
-        compiler_params=pltpu.CompilerParams(collective_id=1, has_side_effects=True, vmem_limit_bytes=60 << 20),
-        name="scatter",
-    )(part, minor, corr)
-
-
-def finish_kernel(n_heads, total, minor, corr, ing, output, up, down, conv_w, conv_b, maps, gate_w, gate_b, group, skip, gain, ing_out, out):
+def finish_kernel(n_heads, x, og, norm_gain, up_total, down_total, minor, corr, ng, output,
+                  up, down, conv_w, conv_b, maps, gate_w, gate_b, group, skip, gain, ing, out):
+    step = pl.program_id(0)
+    rows = x.shape[0]
+    out[...] = output[...]
+    unit, inv_std = normalised(x[...].astype(F32))
+    follows = jnp.where((lax.axis_index("head") < n_heads - 1) & (step == pl.num_programs(0) - 1), 1.0, 0.0)
+    grads = ng[...] + jnp.concatenate([jnp.zeros((rows - HALO, x.shape[1]), F32), corr[...] * follows], axis=0)
+    scaled = grads * jnp.concatenate([norm_gain[j : j + 1] for j in range(norm_gain.shape[0])], axis=1)
+    ing[...] = og[...].astype(F32) + inv_std * (
+        scaled - jnp.mean(scaled, axis=1, keepdims=True) - unit * jnp.mean(scaled * unit, axis=1, keepdims=True)
+    )
+
+    @pl.when(step == 0)
+    def _():
+        finish_small(up_total, down_total, minor, up, down, conv_w, conv_b, maps, gate_w, gate_b, group, skip, gain)
+
+
+def finish_small(up_total, down_total, minor, up, down, conv_w, conv_b, maps, gate_w, gate_b, group, skip, gain):
     dh = minor.shape[1]
-    up[:, 0] = total[:, 0:dh]
-    up[:, 1] = total[:, dh : 2 * dh]
-    down[...] = total[:, 2 * dh :]
+    up[:, 0] = up_total[:, 0:dh]
+    up[:, 1] = up_total[:, dh : 2 * dh]
+    down[...] = down_total[...]
     conv_w[...] = minor[0:TAPS]
     for j in range(dh // 128):
         at = slice(128 * j, 128 * j + 128)
@@ -1013,24 +1123,24 @@
             maps[m, i] = rows[8 * m : 8 * m + 4, 0 : dh // 4]
     gate_b[0:1, 0:1] = minor[10:11, 0:1]
     gate_b[0:1, 1:2] = minor[66:67, 0:1]
-    last = lax.axis_index("head") == n_heads - 1
-    ing_out[...] = ing[...] + jnp.where(last, 0.0, corr[...])
 
 
 class Chain:
-    def __init__(self, by, retain, linked, leaving, landed, sems):
+    def __init__(self, by, retain, linked, leaving, landed, sems, carried=None):
         self.dp, head = lax.axis_index("dp"), lax.axis_index("head")
         self.heads = lax.axis_size("head")
         self.ahead, self.behind = lax.rem(head + 1, self.heads), lax.rem(head + self.heads - 1, self.heads)
         self.place = head if by > 0 else self.heads - 1 - head
         self.to = (self.dp, self.ahead if by > 0 else self.behind)
         self.retain, self.linked, self.leaving, self.landed, self.sems = retain, linked, leaving, landed, sems
+        self.carried = carried or range(self.heads)
+        self.base = self.carried[0]
 
     def greet(self):
         greet([(self.dp, self.ahead), (self.dp, self.behind)])
 
     def copy(self, i):
-        return remote(self.leaving.at[i], self.landed.at[i], self.sems, i, self.to)
+        return remote(self.leaving.at[i - self.base], self.landed.at[i], self.sems, i, self.to)
 
     def pump(self, i):
         @pl.when(self.place != 0)
@@ -1038,7 +1148,8 @@
             self.copy(i).wait_recv()
             entering = self.landed[i].astype(F32) * self.linked
             self.landed[i] = entering.astype(BF16)
-            self.leaving[i] = (self.leaving[i].astype(F32) + entering * self.retain[i, 0:1, 0:1]).astype(BF16)
+            own = self.leaving[i - self.base].astype(F32)
+            self.leaving[i - self.base] = (own + entering * self.retain[i, 0:1, 0:1]).astype(BF16)
 
         @pl.when(self.place == 0)
         def _():
@@ -1051,7 +1162,7 @@
     def finish(self):
         @pl.when(self.place != self.heads - 1)
         def _():
-            for i in range(self.heads):
+            for i in self.carried:
                 self.copy(i).wait_send()
 
 
@@ -1094,7 +1205,8 @@
     sem = pltpu.SemaphoreType.DMA((H,))
     state = pltpu.VMEM((H, srows, dh), BF16)
     late = lambda a: (a, sp.cols("second", n, dh))
-    output, gcol, grow, retain, dng, sttot, gloc, gend, gaug, ogg, dskip, sums = call(
+    first = H // 2
+    output, gcol, grow, retain, dng, sttot, gloc, gend, gaug, ogg, dskip, sums, gin = call(
         partial(forward_kernel, H, log_scale), "forward", 2,
         [whole(inputs), whole(out_grad), whole(gates), whole(flags), late(q), (k, sp.cols("both", n, dh)),
          (va, sp.lead("both", n, dh + 128)), late(og), late(pre), (pack, sp.lead("second", *pack.shape[1:])),
@@ -1105,52 +1217,76 @@
          (sds((H, nch - 1, srows, dh), BF16), sp.lead("second", nch - 1, srows, dh)),
          (sds((H, srows, dh), BF16), sp.lead("second", srows, dh)),
          (sds((H, n, dh + 128), BF16), sp.lead("second", n, dh + 128)), late(sds((H, n, dh), BF16)),
-         late(sds((H, n, dh), BF16)), (sds((H, 8, dh), F32), sp.lead("second", 8, dh))],
+         late(sds((H, n, dh), BF16)), (sds((H, 8, dh), F32), sp.lead("second", 8, dh)),
+         whole(sds((first, srows, dh), BF16))],
         [pltpu.VMEM((n, d), F32), pltpu.VMEM((d, n), BF16), pltpu.VMEM((n, dh + 128), F32), pltpu.VMEM((n, dh), BF16),
          pltpu.VMEM((dh + 128, dh), BF16), pltpu.VMEM((dh, dh), F32), pltpu.VMEM((1, dh), F32),
-         pltpu.VMEM((H, nch - 1, srows, dh), BF16), state, state, pltpu.VMEM((H, 8, 128), F32), sem, sem],
+         pltpu.VMEM((H, nch - 1, srows, dh), BF16), state, state, pltpu.VMEM((H, 8, 128), F32), sem, sem,
+         pltpu.VMEM((first, srows, dh), BF16), pltpu.VMEM((first, srows, dh), BF16), pltpu.SemaphoreType.DMA((first,)),
+         pltpu.SemaphoreType.DMA((first,))],
         collective_id=2, has_side_effects=True,
     )
 
     early = lambda a, *shape: (a, sp.lead("first", *shape))
-    grads, ing, corr, minor = call(
-        partial(backward_kernel, H, log_scale), "backward", 2,
-        [whole(inputs), whole(halo), whole(gain), whole(flags), whole(out_grad), whole(normt), whole(gates), whole(gcol),
-         whole(grow), whole(retain), whole(gend), (q, sp.cols("both", n, dh)), (k, sp.cols("both", n, dh)),
-         (va, sp.lead("both", n, dh + 128)), early(gaug, n, dh + 128), early(sttot, nch, srows, dh),
-         early(gloc, nch - 1, srows, dh), late(pre), (br, sp.cols("second", n + HALO, dh)), late(ogg), late(dskip),
-         (pack, sp.lead("second", *pack.shape[1:])), (w_all, sp.lead("second", d, 2 * dh)),
-         (dng, sp.lead("second", d, dh)), (sums, sp.lead("second", 8, dh))],
-        [(sds((H, d, 3 * dh), BF16), sp.lead("second", d, 3 * dh)), whole(sds((n, d), F32)), whole(sds((HALO, d), F32)),
-         whole(sds((H, 72, dh), F32))],
-        [pltpu.VMEM((H, n, dh), BF16), pltpu.VMEM((H, n, dh), BF16), pltpu.VMEM((H, n, dh), BF16),
-         pltpu.VMEM((n, 128), BF16), pltpu.VMEM((8, 128), F32),
-         pltpu.VMEM((dh + 128, dh), BF16), pltpu.VMEM((dh + 128, dh), BF16), pltpu.VMEM((n, 128), F32),
-         pltpu.VMEM((128, n), F32), pltpu.VMEM((8, 128), F32),
-         pltpu.VMEM((HALO, d), F32), pltpu.VMEM((n + 2 * HALO, dh), F32), pltpu.VMEM((n + HALO, dh), F32),
-         pltpu.VMEM((n, 2 * dh), BF16), pltpu.VMEM((n, dh), BF16), pltpu.VMEM((dh // 128, 128, 256), BF16), pltpu.VMEM((dh // 128, 128, 128), BF16),
-         pltpu.VMEM((3, 128, dh), BF16), state, state, sem, sem],
-        collective_id=3, has_side_effects=True,
-    )
-
-    total, minor, corr = scattered(grads, minor, corr)
-    rows = total.shape[0]
+    turn = lambda a, *shape: (a, sp.lead("turned", *shape))
+    late = lambda a: (a, sp.cols("turned", *a.shape[1:]))
+    rows = up_weight.shape[0]
+    inside = by_hand(rows)
+    anywhere = pl.BlockSpec(memory_space=pl.ANY)
+    vmem = pltpu.VMEM
+    ins = [whole(halo), whole(gain), whole(flags), whole(normt), whole(gates), whole(gcol), whole(grow), whole(retain),
+           (gend, pl.BlockSpec((H - first, srows, dh), lambda s: (1, 0, 0), pipeline_mode=pl.Buffered(1))), whole(gin), (q, sp.cols("mixed", n, dh)), (k, sp.cols("mixed", n, dh)), (va, sp.lead("mixed", n, dh + 128)),
+           early(gaug, n, dh + 128), early(sttot, nch, srows, dh), early(gloc, nch - 1, srows, dh),
+           late(pre), late(br), late(ogg), late(dskip), turn(pack, *pack.shape[1:]), turn(w_all, d, 2 * dh),
+           turn(sums, 8, dh)]
+    sums_here = [sds((H, 72, dh), F32), sds((HALO, d), F32)]
+    scratch = [vmem((H, n, dh), BF16), vmem((H, n, dh), BF16), vmem((H, n, dh), BF16), vmem((n, 128), BF16),
+               vmem((8, 128), F32), vmem((dh + 128, dh), BF16), vmem((dh + 128, dh), BF16), vmem((n, 128), F32),
+               vmem((128, n), F32), vmem((8, 128), F32), vmem((n + 2 * HALO, dh), F32), vmem((n, 2 * dh), BF16),
+               vmem((n, dh), BF16), vmem((dh // 128, 128, 256), BF16), vmem((dh // 128, 128, 128), BF16),
+               vmem((3, 128, dh), BF16), vmem((d, 128), F32), vmem((H - first, srows, dh), BF16), state, sem, sem]
+    if inside:
+        ins.append((dng, anywhere))
+        outs = [sds((rows, 2 * dh), F32), sds((rows, dh), F32), sds((72, dh), F32), sds((HALO, d), F32), sds((n, d), F32)]
+        small = lambda count: vmem((count, 72, dh), F32)
+        dma = pltpu.SemaphoreType.DMA
+        scratch += [vmem((d, 2 * dh), BF16), vmem((H, 72, dh), F32), vmem((HALO, d), F32), vmem((HALO, d), F32), small(2), small(3), small(2),
+                    small(4), dma((2,)), dma((7,)), dma((7,)), *Scatter.scratch(d, rows, 2 * dh),
+                    *Scatter.scratch(d, rows, dh)]
+        outs = [whole(o) for o in outs]
+    else:
+        outs = [(sds((H, d, 2 * dh), BF16), sp.cols("turned", d, 2 * dh)), *(whole(o) for o in sums_here),
+                whole(sds((n, d), F32))]
+    made = call(partial(backward_kernel, inside, H, log_scale), "backward", 2, ins, outs, scratch,
+                collective_id=3, has_side_effects=True)
+    if inside:
+        up_total, down_total, minor, corr, ng = made
+    else:
+        upg, minor, corr, ng = made
+
+        def summed(part):
+            part = lax.psum_scatter(part, "head", scatter_dimension=0, tiled=True)
+            return lax.psum_scatter(part, "dp", scatter_dimension=1, tiled=True)[0].astype(F32)
+
+        up_total, down_total = summed(upg), summed(dng)
+        minor = lax.psum(lax.psum_scatter(minor, "head", scatter_dimension=0, tiled=True), "dp")[0]
+        corr = shifted(corr, -1)
+
     once = lambda *shape: pl.BlockSpec(shape, lambda i: (0,) * len(shape))
-    tail = pl.BlockSpec((HALO, d), lambda i: (n // HALO - 1, 0))
+    chunk = pl.BlockSpec((CH, d), lambda i: (i, 0))
     lines = (dh // 128, 128)
     shapes = [(rows, 2, dh), (rows, dh), (TAPS, dh), lines, (3, 4, 4, dh // 4), (3, 2 * H, dh), (1, 2), lines, lines,
               (d // 128, 128)]
-    anywhere = pl.BlockSpec(memory_space=pl.ANY)
-    up, down, conv_w, conv_b, maps, gate_w, gate_b, group, skip, gain, ing, output = pl.pallas_call(
+    up, down, conv_w, conv_b, maps, gate_w, gate_b, group, skip, norm, ing, output = pl.pallas_call(
         partial(finish_kernel, H),
-        grid=(1,),
+        grid=(n // CH,),
         out_shape=[*(sds(shape, F32) for shape in shapes), sds((n, d), F32), sds((n, d), BF16)],
-        in_specs=[once(*total.shape), once(*minor.shape), once(*corr.shape), tail, anywhere],
-        out_specs=[*(once(*shape) for shape in shapes), tail, anywhere],
-        input_output_aliases={3: 10, 4: 11},
+        in_specs=[chunk, chunk, *(once(*a.shape) for a in (gain, up_total, down_total, minor, corr)), chunk, chunk],
+        out_specs=[*(once(*shape) for shape in shapes), chunk, chunk],
+        compiler_params=params(),
         name="finish",
-    )(total, minor, corr, ing, output)
-    return (output, ing, gain.reshape(d), up, conv_w, conv_b.reshape(dh), maps.transpose(0, 3, 1, 2),
+    )(inputs, out_grad, gain, up_total, down_total, minor, corr, ng, output)
+    return (output, ing, norm.reshape(d), up, conv_w, conv_b.reshape(dh), maps.transpose(0, 3, 1, 2),
             gate_w.transpose(0, 2, 1), gate_b.T, group.reshape(dh), skip.reshape(dh), down.T)
 
 

time: 260 us -> 239 us (0.919); the launches traced: 258 us -> 240 us
  Pallas kernels: 252 us -> 239 us
  local copies, waits for them, and re-layouts: 4.47 us -> 0 us
    pallas_call x2 -> x1, Pallas kernels: 51.9 us -> 7.76 us  [local(): pl.pallas_call(partial(finish_kernel, H), grid=(n // CH,), out_shape=[*(s...]
    pallas_call x3, Pallas kernels: 155 us -> 186 us  [call(): pl.pallas_call(kernel, grid=(H * rounds,), out_shape=[o[0] for o in outs]...]
    unnamed x4 -> x0, local copies, waits for them, and re-layouts: 4.47 us -> none
where the time goes in v1:
time: 239 us; the launch traced here: 240 us
  Pallas kernels  239 us (100%)
    pallas_call x3, Pallas kernels, call(): pl.pallas_call(kernel, grid=(H * rounds,), out_shape=[o[0] for o in outs]...  186 us
    pallas_call x1, Pallas kernels, gathered(): pl.pallas_call(gather_kernel, out_shape=[sds((heads, dp * rows, 3 * dh),...  45.3 us
    pallas_call x1, Pallas kernels, local(): pl.pallas_call(partial(finish_kernel, H), grid=(n // CH,), out_shape=[*(s...  7.76 us

profile of v1, /device:TPU:0, one launch (start us, length us, event | category | flops | bytes accessed | tf_op | source)
XLA Modules:
  0.0 239.8 jit_solution(5144225218658006031)
XLA Ops:
  0.6 45.3 %gather.1 = (bf16[4,768,1152]{2,1,0:T(8,128)(2,1)}, f32[4,48,384]{2,1,0:T(8,128)}, bf16[16,768]{1,0:T(8,128)(2,1)}) custom-call(bf16[96,2,384]{2,1,0:T(2,128)(2,1)} %up_raw.1, bf16[96,384]{1,0:T(8,128)(2,1)} %bitcast.17, f32[4,384]{1,0:T(4,128)} %taps.1, f32[3,128]{1,0:T(4,128)} %bitcast.24, f32[3,128]{1,0:T(4,128)} %bitcast.25, f32[3,128]{1,0:T(4,128)} %bitcast.26, ...), custom_call_target="tpu_custom_call" | custom-call | tf_op jit(solution)/shard_map/gather/pallas_call | solution.py:1071
  46.0 23.2 %lift.1 = (bf16[4,1024,384]{2,1,0:T(8,128)(2,1)}, bf16[4,1024,384]{2,1,0:T(8,128)(2,1)}, bf16[4,1024,512]{2,1,0:T(8,128)(2,1)}, bf16[4,1024,384]{2,1,0:T(8,128)(...) custom-call(bf16[1024,768]{1,0:T(8,128)(2,1)} %x.3, ...), custom_call_target="tpu_custom_call" | custom-call | tf_op jit(solution)/shard_map/lift/pallas_call | solution.py:1185
  69.1 51.7 %forward.1 = (bf16[1024,768]{1,0:T(8,128)(2,1)}, f32[1024,128]{1,0:T(8,128)}, f32[8,1024]{1,0:T(8,128)}, f32[4,8,128]{2,1,0:T(8,128)}, bf16[4,768,384]{2,1,0:T(8...) custom-call(bf16[1024,768]{1,0:T(8,128)(2,1)} %x.3, ...), custom_call_target="tpu_custom_call" | custom-call | tf_op jit(solution)/shard_map/forward/pallas_call | solution.py:1185
  120.9 111.0 %backward.1 = (f32[96,768]{1,0:T(8,128)}, f32[96,384]{1,0:T(8,128)}, f32[72,384]{1,0:T(8,128)}, f32[16,768]{1,0:T(8,128)}, f32[1024,768]{1,0:T(8,128)}) custom-call(bf16[16,768]{1,0:T(8,128)(2,1)} %get-tuple-element.54.halo_ref, f32[6,128]{1,0:T(8,128)} %bitcast.19, f32[16,128]{1,0:T(8,128)} %get-tuple-element.57.flags_ref, ...), custom_call_target="tpu_custom_call" | custom-call | tf_op jit(solution)/shard_map/backward/pallas_call | solution.py:1185
  231.9 7.8 %finish.1 = (f32[96,2,384]{2,1,0:T(2,128)}, f32[96,384]{1,0:T(8,128)}, f32[4,384]{1,0:T(4,128)}, f32[3,128]{1,0:T(4,128)}, f32[3,4,4,96]{3,2,1,0:T(4,128)}, /*in...) custom-call(bf16[1024,768]{1,0:T(8,128)(2,1)} %x.3, ...), custom_call_target="tpu_custom_call" | custom-call | tf_op jit(solution)/shard_map/finish/pallas_call | solution.py:1280
